TPU v7x, 256 devices: a whole 4x4x8 slice. The times are simulated.
256 devices in a mesh: tm: 32 (over z, x), space: 8 (over y, core).
Axes of the slice: x: 4, y: 4, z: 8, core: 2. Of those that a mesh axis runs over, the one named last changes fastest.
Arguments:
- frames: bfloat16 [128, 32, 128, 128], P('tm', 'space'), may hold values from -6 to 6
- conv_weight: bfloat16 [3456, 128], replicated, may hold values from -0.109375 to 0.109375
- conv_bias: float32 [128], replicated, may hold values from -3 to 3
- projection: float32 [128, 6], replicated, may hold values from -1 to 1
- levels: int32 [6], replicated, may hold values from 3 to 8, as said below
- centres: int32 [32, 32, 768], P(None, 'space', 'tm'), may hold values from 0 to 7, as said below
- code_grad: float32 [32, 32, 768], P(None, 'space', 'tm'), may hold values from -6 to 6
Outputs:
- quantized: float32 [32, 32, 768], P(None, 'space', 'tm')
- weight_grad: float32 [3456, 128], P('tm', 'space')
- projection_grad: float32 [128, 6], replicated
- bias_grad: float32 [128], replicated
Inputs may be any that keep to these rules, and one draw needn't show every extreme that they name: Level counts of the FSQ channels; in every draw some channel has 3 levels and some has 8. centres[g, h, q] is below levels[q % 6].
All inputs are finite; a program needn't handle non-finite values.
Results may differ from a plain program's by a relative error of at most 0.0024.
Values may be sent and summed in bfloat16 or wider, within the bound.
No kernel may reach another device: no remote copies, remote signals or barrier semaphores. Data moves between devices by JAX's collectives and lax.ppermute only.
A program may use at most 64 MiB of HBM per device.

v0:
```python
import jax
import jax.numpy as jnp
from jax import lax
from jax.sharding import PartitionSpec as P

offset_scale = 0.45
commit_weight = 0.25
highest = lax.Precision.HIGHEST


def passed_along(value, axis, steps):
    count = lax.axis_size(axis)
    first, last = (max(0, -steps), min(count, count - steps))
    return lax.ppermute(value, axis, [(source, source + steps) for source in range(first, last)])


def extended(block, sides, width):
    for axis, dim in sides:
        count = lax.axis_size(axis)
        forward = [(i, i + 1) for i in range(count - 1)]
        backward = [(target, source) for source, target in forward]
        low = lax.ppermute(
            lax.slice_in_dim(block, block.shape[dim] - width, None, axis=dim), axis, forward
        )
        high = lax.ppermute(lax.slice_in_dim(block, 0, width, axis=dim), axis, backward)
        block = jnp.concatenate([low, block, high], axis=dim)
    return block


def widen_columns(bordered):
    frame_width = bordered.shape[2]
    padded = jnp.pad(bordered, ((0, 0), (0, 0), (1, 1), (0, 0)))
    return jnp.concatenate(
        [padded[:, :, column_shift : column_shift + frame_width] for column_shift in range(3)],
        axis=3,
    )


def tap_slabs(widened, frame_count, row_count):
    triple = widened.shape[3]
    slabs = []
    for time_tap in range(3):
        for row_tap in range(3):
            slabs.append(
                widened[time_tap : time_tap + frame_count, row_tap : row_tap + row_count].reshape(
                    -1, triple
                )
            )
    return slabs


def on_device(frames, conv_weight, conv_bias, projection, levels, centres, code_grad):
    frame_count, row_count, frame_width, channels = frames.shape
    first_device = lax.axis_index("tm") == 0
    received = passed_along(frames[frame_count - 2 :], "tm", 1)
    earlier = jnp.where(first_device, jnp.broadcast_to(frames[:1], received.shape), received)
    bordered = extended(jnp.concatenate([earlier, frames], 0), (("space", 1),), 1)
    slabs = tap_slabs(widen_columns(bordered), frame_count, row_count)
    triple = 3 * channels
    cell_count = row_count * frame_width
    preact = jnp.zeros((frame_count * cell_count, channels), jnp.float32) + conv_bias
    for tap_number in range(9):
        preact = preact + jnp.dot(
            slabs[tap_number],
            conv_weight[tap_number * triple : (tap_number + 1) * triple],
            preferred_element_type=jnp.float32,
        )
    activated = lax.optimization_barrier(jax.nn.silu(preact).astype(jnp.bfloat16))
    group_count = frame_count // 4
    pooled = (
        activated.astype(jnp.float32).reshape(group_count, 4, cell_count, channels).sum(1) * 0.25
    )
    latent_count = levels.shape[0]
    latent = jnp.dot(pooled, projection, precision=highest).reshape(
        group_count, row_count, frame_width * latent_count
    )
    tiled_latent = lax.all_to_all(latent, "tm", split_axis=2, concat_axis=0, tiled=True)
    half_range = (levels.astype(jnp.float32) - 1.0) * 0.5
    half_column = jnp.tile(half_range, tiled_latent.shape[2] // latent_count)
    quantized = (centres.astype(jnp.float32) - half_column) / half_column
    squashed = jnp.tanh(tiled_latent)
    total_cells = 4 * tiled_latent.shape[0] * row_count * lax.axis_size("space") * frame_width
    tile_step = (
        (code_grad / half_column + 2.0 * commit_weight * offset_scale * squashed)
        * offset_scale
        * (1.0 - squashed * squashed)
        * float(total_cells) ** (-0.5)
    )
    code_step = lax.all_to_all(tile_step, "tm", split_axis=0, concat_axis=2, tiled=True).reshape(
        group_count, cell_count, latent_count
    )
    projection_part = jnp.einsum("gnc,gnl->cl", pooled, code_step, precision=highest)
    pooled_grad = jnp.dot(code_step, projection.T, precision=highest)
    sigmoid_pre = jax.nn.sigmoid(preact)
    silu_slope = sigmoid_pre * (1.0 + preact * (1.0 - sigmoid_pre))
    pre_grad = (
        0.25 * pooled_grad[:, None] * silu_slope.reshape(group_count, 4, cell_count, channels)
    ).reshape(-1, channels)
    bias_part = pre_grad.sum(0)
    low_grad = pre_grad.astype(jnp.bfloat16)
    weight_sum = jnp.concatenate(
        [
            lax.dot_general(
                tap_slab, low_grad, (((0,), (0,)), ((), ())), preferred_element_type=jnp.float32
            )
            for tap_slab in slabs
        ],
        0,
    )
    column_part = lax.psum_scatter(weight_sum, "space", scatter_dimension=1, tiled=True)
    weight_grad = lax.psum_scatter(column_part, "tm", scatter_dimension=0, tiled=True)
    projection_grad, bias_grad = lax.psum((projection_part, bias_part), ("tm", "space"))
    return (quantized, weight_grad, projection_grad, bias_grad)


def solution(mesh):
    return jax.shard_map(
        on_device,
        mesh=mesh,
        in_specs=(
            P("tm", "space", None, None),
            P(),
            P(),
            P(),
            P(),
            P(None, "space", "tm"),
            P(None, "space", "tm"),
        ),
        out_specs=(P(None, "space", "tm"), P("tm", "space"), P(), P()),
        check_vma=False,
    )
```

profile of v0, /device:TPU:2, one launch (start us, length us, event | category | flops | bytes accessed | tf_op | source)
XLA Modules:
  0.0 313.0 jit_solution(7041506376916107857)
XLA Ops:
  7.2 1.0 slice.74
  8.2 3.4 %collective-permute-start = (bf16[2,4,128,128]{3,2,1,0:T(8,128)(2,1)S(1)}, bf16[2,4,128,128]{3,2,1,0:T(8,128)(2,1)S(1)}, u32[]{:S(2)}, u32[]{:S(2)}) collective-permute-start(bf16[2,4,128,128]{3,2,1,0:T(8,128)(2,1)S(1)} %slice.74), channel_id=1, source_target_pairs={{0,8},{8,16},{16,24},{24,32},{32,40},{40,48},{48,56},{56,64},{64,7... | collective-permute-start | bytes 786440 | tf_op jit(solution)/shard_map/ppermute | solution.py:14
  11.6 0.9 slice_bitcast_fusion
  12.6 5.6 %collective-permute-done = bf16[2,4,128,128]{3,2,1,0:T(8,128)(2,1)S(1)} collective-permute-done((bf16[2,4,128,128]{3,2,1,0:T(8,128)(2,1)S(1)}, bf16[2,4,128,128]{3,2,1,0:T(8,128)(2,1)S(1)}, u32[]{:S(2)}, u32[]{:S(2)}) %collective-permute-start) | collective-permute-done | bytes 262176 | tf_op jit(solution)/shard_map/ppermute | solution.py:14
  18.2 1.3 collective-permute-start.1
  19.6 1.3 collective-permute-start.2
  20.9 3.8 %collective-permute-done.2 = bf16[6,1,128,128]{3,2,1,0:T(8,128)(2,1)S(1)} collective-permute-done((bf16[6,1,128,128]{3,2,1,0:T(8,128)(2,1)S(1)}, bf16[6,1,128,128]{3,2,1,0:T(8,128)(2,1)S(1)}, u32[]{:S(2)}, u32[]{:S(2)}) %collective-permute-start.2) | collective-permute-done | bytes 196640 | tf_op jit(solution)/shard_map/ppermute | solution.py:25
  24.7 0.5 select_maximum_fusion
  25.2 0.7 fusion.42
  25.9 0.6 pad_maximum_fusion
  26.5 2.7 fusion.41
  29.3 0.6 fusion.19
  29.9 0.6 fusion.21
  30.5 0.6 fusion.23
  31.1 0.6 fusion.25
  31.7 0.6 fusion.27
  32.3 0.6 fusion.29
  32.8 0.6 fusion.31
  33.4 0.6 fusion.33
  34.1 1.9 multiply_convert_fusion
  36.1 1.1 fusion.15
  37.2 1.1 reshape.101
  38.3 1.0 copy.30
  39.3 12.5 %all-to-all-start = ((f32[1,4,768]{1,0,2:T(1,128)}), f32[1,4,768]{1,0,2:T(1,128)}, u32[]{:S(2)}, u32[]{:S(2)}) async-start(f32[1,4,768]{1,0,2:T(1,128)} %copy.30), calls=%async_computation | async-start | bytes 786432 | tf_op jit(solution)/shard_map/all_to_all | solution.py:77
  51.9 0.1 copy.27
  52.0 1.5 copy.28
  53.5 0.1 sub.29
  53.6 10.5 %all-to-all-done = f32[1,4,768]{1,0,2:T(1,128)} async-done(((f32[1,4,768]{1,0,2:T(1,128)}), f32[1,4,768]{1,0,2:T(1,128)}, u32[]{:S(2)}, u32[]{:S(2)}) %all-to-all-start) | async-done | bytes 12320 | tf_op jit(solution)/shard_map/all_to_all | solution.py:77
  64.1 1.1 copy.31
  65.2 0.7 mul.89
  66.0 0.7 reshape.106
  66.7 0.9 fusion.36
  67.7 15.2 %all_to_all.24 = f32[32,4,24]{2,1,0:T(4,128)S(1)} all-to-all(f32[32,4,24]{2,1,0:T(4,128)S(1)} %copy.32), channel_id=1, replica_groups=mesh['tm'=32,'space'=8] {'tm'}, dimensions={0} | all-to-all | bytes 24576 | tf_op jit(solution)/shard_map/all_to_all | solution.py:89
  82.9 0.8 reshape.102
  83.7 1.4 convolution_multiply_fusion
  85.1 1.7 fusion.40
  86.8 1.3 convolution_dynamic-update-slice_fusion.8
  88.1 0.1 copy-done.12
  88.2 1.3 convolution_dynamic-update-slice_fusion.7
  89.5 0.1 copy-done.10
  89.6 1.3 convolution_dynamic-update-slice_fusion.6
  90.9 0.1 copy-done.8
  91.0 1.3 convolution_dynamic-update-slice_fusion.5
  92.3 0.1 copy-done.6
  92.4 1.3 convolution_dynamic-update-slice_fusion.4
  93.7 0.1 copy-done.4
  93.8 1.3 convolution_dynamic-update-slice_fusion.3
  95.1 0.1 copy-done.2
  95.2 1.3 convolution_dynamic-update-slice_fusion.2
  96.5 1.3 convolution_dynamic-update-slice_fusion.1
  97.8 1.3 convolution_dynamic-update-slice_fusion
  99.1 2.7 copy.37
  101.8 0.7 copy-done.20
  102.5 0.6 dynamic-slice.4
  103.7 0.7 copy.34
  104.4 33.0 %reduce-scatter.6.cloned.1.call-done = f32[16,3456]{1,0:T(8,128)} async-done(((f32[128,3456]{1,0:T(8,128)}), f32[16,3456]{1,0:T(8,128)}) %reduce-scatter.6.cloned.1.call-update) | async-done | bytes 221200
  137.5 1.5 copy.38
  139.0 84.0 %fusion = f32[112,16]{1,0:T(8,128)S(1)} fusion(f32[3456,16]{1,0:T(8,128)S(1)} %copy.38), kind=kCustom, calls=%all-reduce-scatter | all-reduce-scatter fusion | flops 57345 | bytes 229376
  223.0 1.9 collective-permute-start.3
  224.9 0.5 fusion.13
  225.5 2.0 collective-permute-start.4
  227.5 77.5 %all-reduce.3 = (f32[128,6]{0,1:T(8,128)}, f32[128]{0:T(128)}) all-reduce(f32[128,6]{0,1:T(8,128)S(1)} %fusion.13, f32[128]{0:T(128)S(1)} %get-tuple-element.22), channel_id=1, replica_groups=mesh['tm'=32,'space'=8] {'tm','space'}, use_global_device_ids=true, to_apply=%region_3.4 | all-reduce | flops 896 | bytes 7168 | tf_op jit(solution)/shard_map/psum | solution.py:112
  305.0 0.4 concatenate.16
  305.5 0.7 copy.35
  (52 shorter events, 0.4 us)
Async XLA Ops:
  7.2 28.9 %copy-start = (f32[128,6]{0,1:T(8,128)S(1)}, f32[128,6]{0,1:T(8,128)}, u32[]{:S(2)}) copy-start(f32[128,6]{0,1:T(8,128)} %param.10) | copy-start | bytes 9220
  7.2 11.0 %copy-start.15 = (bf16[4,4,128,128]{3,2,1,0:T(8,128)(2,1)S(1)}, bf16[4,4,128,128]{3,2,1,0:T(8,128)(2,1)}, u32[]{:S(2)}) copy-start(bf16[4,4,128,128]{3,2,1,0:T(8,128)(2,1)} %param.7) | copy-start | bytes 1572868
  8.2 9.9 %collective-permute-start = (bf16[2,4,128,128]{3,2,1,0:T(8,128)(2,1)S(1)}, bf16[2,4,128,128]{3,2,1,0:T(8,128)(2,1)S(1)}, u32[]{:S(2)}, u32[]{:S(2)}) collective-permute-start(bf16[2,4,128,128]{3,2,1,0:T(8,128)(2,1)S(1)} %slice.74), channel_id=1, source_target_pairs={{0,8},{8,16},{16,24},{24,32},{32,40},{40,48},{48,56},{56,64},{64,7... | collective-permute-start | bytes 786440 | tf_op jit(solution)/shard_map/ppermute | solution.py:14
  18.2 2.6 collective-permute-start.1
  19.6 5.1 %collective-permute-start.2 = (bf16[6,1,128,128]{3,2,1,0:T(8,128)(2,1)S(1)}, bf16[6,1,128,128]{3,2,1,0:T(8,128)(2,1)S(1)}, u32[]{:S(2)}, u32[]{:S(2)}) collective-permute-start(bf16[6,1,128,128]{3,2,1,0:T(8,128)(2,1)S(1)} %get-tuple-element.36), channel_id=1, source_target_pairs={{1,0},{2,1},{3,2},{4,3},{5,4},{6,5},{7,6},{9,8},{10,9},{11,10},{12... | collective-permute-start | bytes 589832 | tf_op jit(solution)/shard_map/ppermute | solution.py:25
  26.5 2.8 copy-start.17
  29.2 1.2 copy-start.1
  29.3 1.8 copy-start.3
  29.3 2.4 copy-start.5
  29.3 3.0 copy-start.7
  29.3 3.6 %copy-start.9 = (bf16[4,4,128,384]{3,2,1,0:T(8,128)(2,1)}, bf16[4,4,128,384]{3,2,1,0:T(8,128)(2,1)S(1)}, u32[]{:S(2)}) copy-start(bf16[4,4,128,384]{3,2,1,0:T(8,128)(2,1)S(1)} %get-tuple-element.31) | copy-start | bytes 4718596
  29.3 4.1 %copy-start.11 = (bf16[4,4,128,384]{3,2,1,0:T(8,128)(2,1)}, bf16[4,4,128,384]{3,2,1,0:T(8,128)(2,1)S(1)}, u32[]{:S(2)}) copy-start(bf16[4,4,128,384]{3,2,1,0:T(8,128)(2,1)S(1)} %get-tuple-element.24) | copy-start | bytes 4718596
  29.3 4.7 %copy-start.13 = (bf16[4,4,128,384]{3,2,1,0:T(8,128)(2,1)}, bf16[4,4,128,384]{3,2,1,0:T(8,128)(2,1)S(1)}, u32[]{:S(2)}) copy-start(bf16[4,4,128,384]{3,2,1,0:T(8,128)(2,1)S(1)} %get-tuple-element.32) | copy-start | bytes 4718596
  33.4 0.7 copy-start.19
  36.0 15.8 %copy-start.21 = (s32[6]{0:T(128)S(1)}, s32[6]{0:T(128)}, u32[]{:S(2)}) copy-start(s32[6]{0:T(128)} %param.11) | copy-start | bytes 76
  36.0 15.9 %copy-start.18 = (s32[32,4,24]{0,2,1:T(8,128)S(1)}, s32[32,4,24]{0,2,1:T(8,128)}, u32[]{:S(2)}) copy-start(s32[32,4,24]{0,2,1:T(8,128)} %param.12) | copy-start | bytes 36868
  39.3 24.8 %all-to-all-start = ((f32[1,4,768]{1,0,2:T(1,128)}), f32[1,4,768]{1,0,2:T(1,128)}, u32[]{:S(2)}, u32[]{:S(2)}) async-start(f32[1,4,768]{1,0,2:T(1,128)} %copy.30), calls=%async_computation | async-start | bytes 786432 | tf_op jit(solution)/shard_map/all_to_all | solution.py:77
  51.8 85.7 %reduce-scatter.6.cloned.1.call-start = ((), (), s32[]{:S(2)}) async-start(), calls=%async_computation.3 | async-start | bytes 1990656
  83.7 3.1 copy-start.14
  86.8 1.4 copy-start.12
  88.2 1.4 copy-start.10
  89.6 1.4 copy-start.8
  91.0 1.4 copy-start.6
  92.4 1.4 copy-start.4
  93.8 1.4 copy-start.2
  101.8 0.7 copy-start.20
  137.5 87.5 %copy-start.16 = (f32[512,6]{1,0:T(8,128)S(1)}, f32[512,6]{1,0:T(8,128)}, u32[]{:S(2)}) copy-start(f32[512,6]{1,0:T(8,128)} %reshape.102) | copy-start | bytes 36868
  223.0 82.0 %collective-permute-start.3 = (f32[112,16]{1,0:T(8,128)S(1)}, f32[112,16]{1,0:T(8,128)S(1)}, u32[]{:S(2)}, u32[]{:S(2)}) collective-permute-start(f32[112,16]{1,0:T(8,128)S(1)} %fusion), channel_id=1, source_target_pairs={{0,8},{8,16},{16,24},{24,32},{32,40},{40,48},{48,56},{56,64},{64,7... | collective-permute-start | bytes 21512
  225.5 79.5 %collective-permute-start.4 = (f32[12,16]{1,0:T(8,128)S(1)}, f32[12,16]{1,0:T(8,128)S(1)}, u32[]{:S(2)}, u32[]{:S(2)}) collective-permute-start(f32[12,16]{1,0:T(8,128)S(1)} %slice.108), channel_id=1, source_target_pairs={{0,16},{8,24},{16,32},{24,40},{32,48},{40,56},{48,64},{56,72},{64,... | collective-permute-start | bytes 2312
Sparse Core Ops, SparseCore 0:
  102.0 35.4 reduce-scatter.5
where the time goes:
time: 317 us; the launch traced here: 313 us
  blocking collectives  177 us (56%)
  waiting for transfers between devices  53 us (17%)
  starting transfers between devices  22.4 us (7%)
  matrix products  21.1 us (7%)
  local copies, waits for them, and re-layouts  20.7 us (7%)
  between operations  15.1 us (5%)
  other arithmetic  3.86 us (1%)
    unnamed x1, blocking collectives  84 us
    psum x1, blocking collectives, on_device(): lax.psum((projection_part, bias_part), ('tm', 'space'))  77.5 us
    unnamed x4, waiting for transfers between devices  33.1 us
    all_to_all x1, blocking collectives, on_device(): lax.all_to_all(tile_step, 'tm', split_axis=0, concat_axis=2, tiled=True)  15.2 us
    all_to_all x1, starting transfers between devices, on_device(): lax.all_to_all(latent, 'tm', split_axis=2, concat_axis=0, tiled=True)  12.5 us
    dot_general x9, matrix products, on_device(): lax.dot_general(tap_slab, low_grad, (((0,), (0,)), ((), ())), preferred_e...  11.6 us
    all_to_all x1, waiting for transfers between devices, on_device(): lax.all_to_all(latent, 'tm', split_axis=2, concat_axis=0, tiled=True)  10.5 us
    unnamed x54, local copies, waits for them, and re-layouts  9.67 us
  transfers between devices with their start and end apart: 7, of which 4 were waited for; matrix products, arithmetic and copies ran while one was open for 1% of the time, Pallas kernels for 0%

commit v1 on v0

v1 whole, which is shorter than its diff:
```python
import jax
import jax.numpy as jnp
from jax import lax
from jax.experimental import pallas as pl
from jax.experimental.pallas import tpu as pltpu
from jax.sharding import PartitionSpec as P

offset_scale = 0.45
commit_weight = 0.25
highest = lax.Precision.HIGHEST
bf16 = jnp.bfloat16
f32 = jnp.float32
VMEM_BYTES = 48 * 1024 * 1024
CH = 128
L = 6
W = 128
TAPS = 27
LANES = TAPS * CH
WIDE = LANES + CH


def vmem(count):
    return [pl.BlockSpec(memory_space=pltpu.VMEM)] * count


def call(kernel, out_shape, in_specs, scratch=()):
    outs = len(out_shape)
    return pl.pallas_call(
        kernel,
        out_shape=out_shape,
        in_specs=in_specs,
        out_specs=vmem(outs),
        scratch_shapes=list(scratch),
        compiler_params=pltpu.CompilerParams(vmem_limit_bytes=VMEM_BYTES),
    )


def half_ranges(levels_ref, channel):
    half = jnp.ones(channel.shape, f32)
    for j in range(L):
        half = jnp.where(channel == j, (levels_ref[j].astype(f32) - 1.0) * 0.5, half)
    return half


def code_kernel(levels_ref, centres_ref, grad_ref, quantized_ref, out_ref):
    rows, columns, frames = grad_ref.shape
    channel = lax.broadcasted_iota(jnp.int32, (columns, frames), 0) % L
    half = half_ranges(levels_ref, channel)
    parts = []
    for h in range(rows):
        quantized_ref[h] = (centres_ref[h].astype(f32) - half) / half
        parts.append(grad_ref[h] / half)
    stacked = jnp.concatenate(parts, 0)
    padded = jnp.pad(stacked, ((0, CH - rows * columns), (0, CH - frames)))
    turned = padded.T
    out_ref[...] = turned[:frames]


def shifted_rows(value, step):
    row = lax.broadcasted_iota(jnp.int32, value.shape, 0)
    rolled = pltpu.roll(value, step % value.shape[0], 0)
    edge = 0 if step == 1 else value.shape[0] - 1
    return jnp.where(row == edge, 0.0, rolled)


def shifted_lanes(value, step):
    lane = lax.broadcasted_iota(jnp.int32, value.shape, 1)
    rolled = pltpu.roll(value, step % value.shape[1], 1)
    edge = 0 if step == 1 else value.shape[1] - 1
    return jnp.where(lane == edge, 0.0, rolled)


def block_kernel(
    total_cells,
    frames_ref,
    earlier_ref,
    up_ref,
    down_ref,
    corner_up_ref,
    corner_down_ref,
    weight_ref,
    bias_ref,
    projection_ref,
    code_ref,
    mine_ref,
    theirs_ref,
    x_ref,
    wide_ref,
    slope_ref,
    low_ref,
    grad_ref,
):
    first = lax.axis_index("tm") == 0
    space = lax.axis_index("space")
    core = lax.rem(space, 2)
    row_chip = lax.div(space, 2)
    for t in range(4):
        x_ref[t + 2, 0] = up_ref[t]
        x_ref[t + 2, 5] = down_ref[t]
        for h in range(4):
            x_ref[t + 2, h + 1] = frames_ref[t, h]

    @pl.when(first)
    def _():
        for t in range(2):
            x_ref[t, 0] = up_ref[0]
            x_ref[t, 5] = down_ref[0]
            for h in range(4):
                x_ref[t, h + 1] = frames_ref[0, h]

    @pl.when(jnp.logical_not(first))
    def _():
        for t in range(2):
            x_ref[t, 0] = corner_up_ref[t]
            x_ref[t, 5] = corner_down_ref[t]
            for h in range(4):
                x_ref[t, h + 1] = earlier_ref[t, h]

    for tap in range(9):
        for c in range(3):
            wide_ref[tap * CH : (tap + 1) * CH, c * CH : (c + 1) * CH] = weight_ref[
                (3 * tap + c) * CH : (3 * tap + c + 1) * CH, :
            ]
    bias = bias_ref[...]
    pooled = [jnp.zeros((W, CH), f32) for _ in range(4)]
    for t in range(4):
        for h in range(4):
            left = jnp.concatenate([x_ref[t + a, h + b] for a in range(3) for b in range(3)], 1)
            z = jnp.dot(left, wide_ref[...], preferred_element_type=f32)
            preact = (
                bias
                + shifted_rows(z[:, :CH], 1)
                + z[:, CH : 2 * CH]
                + shifted_rows(z[:, 2 * CH :], -1)
            )
            sigmoid = 1.0 / (1.0 + jnp.exp(-preact))
            slope_ref[t, h] = sigmoid * (1.0 + preact * (1.0 - sigmoid))
            pooled[h] = pooled[h] + (preact * sigmoid).astype(bf16).astype(f32)
    pooled = jnp.concatenate(pooled, 0) * 0.25
    projection = jnp.concatenate([projection_ref[...], jnp.zeros((2, CH), f32)], 0)
    latent = lax.dot_general(
        projection, pooled, (((1,), (1,)), ((), ())), precision=highest, preferred_element_type=f32
    )
    squashed = jnp.tanh(latent)
    tile_of = lax.broadcasted_iota(jnp.int32, (W, 32), 1)
    column = lax.broadcasted_iota(jnp.int32, (W, 32), 0)
    spread = jnp.where(column // 4 == tile_of, 1.0, 0.0).astype(f32)
    repeated = jnp.dot(spread, code_ref[...], precision=highest, preferred_element_type=f32)
    place = lax.broadcasted_iota(jnp.int32, (W, CH), 1)
    column = lax.broadcasted_iota(jnp.int32, (W, CH), 0)
    repeated = jnp.where((place % 24) // L == column % 4, repeated, 0.0)
    wanted = lax.broadcasted_iota(jnp.int32, (32, CH), 0)
    place = lax.broadcasted_iota(jnp.int32, (32, CH), 1)
    pick = jnp.where((place // 24 == wanted // 8) & (place % L == wanted % 8), 1.0, 0.0).astype(f32)
    codes = lax.dot_general(
        pick, repeated, (((1,), (1,)), ((), ())), precision=highest, preferred_element_type=f32
    )
    codes = jnp.concatenate([codes[8 * h : 8 * h + 8] for h in range(4)], 1)
    code_step = (
        (codes + 2.0 * commit_weight * offset_scale * squashed)
        * offset_scale
        * (1.0 - squashed * squashed)
        * float(total_cells) ** (-0.5)
    )
    projection_part = jnp.dot(code_step, pooled, precision=highest, preferred_element_type=f32)
    pooled_grad = 0.25 * lax.dot_general(
        code_step, projection, (((0,), (0,)), ((), ())), precision=highest, preferred_element_type=f32
    )
    bias_part = jnp.zeros((8, CH), f32)
    for t in range(4):
        for h in range(4):
            pre_grad = pooled_grad[h * W : (h + 1) * W] * slope_ref[t, h]
            bias_part = bias_part + pre_grad.reshape(W // 8, 8, CH).sum(0)
            turned = pre_grad.T
            place = (t * 4 + h) * W
            low_ref[0:CH, place : place + W] = shifted_lanes(turned, -1).astype(bf16)
            low_ref[CH : 2 * CH, place : place + W] = turned.astype(bf16)
            low_ref[2 * CH :, place : place + W] = shifted_lanes(turned, 1).astype(bf16)
    bias_row = bias_part.sum(0, keepdims=True)
    row = lax.broadcasted_iota(jnp.int32, (8, CH), 0)
    small = jnp.where(row == L, bias_row, projection_part)
    taps = [(a, b) for a in range(3) for b in range(3)]
    for start in range(0, 9, 2):
        group = taps[start : start + 2]
        right = jnp.concatenate(
            [x_ref[a : a + 4, b : b + 4].reshape(16 * W, CH) for a, b in group], 1
        )
        grad_ref[:, start * CH : (start + len(group)) * CH] = jnp.dot(
            low_ref[...], right, preferred_element_type=f32
        )
    for d in range(4):
        target = 32 * (row_chip ^ d)
        for c in range(3):
            own = pl.multiple_of(c * CH + target + 16 * core, 16)
            other = pl.multiple_of(c * CH + target + 16 * (1 - core), 16)
            for tap in range(9):
                to = slice((3 * tap + c) * CH, (3 * tap + c + 1) * CH)
                mine_ref[d, :, to] = grad_ref[pl.ds(own, 16), tap * CH : (tap + 1) * CH]
                theirs_ref[d, :, to] = grad_ref[pl.ds(other, 16), tap * CH : (tap + 1) * CH]
        mine_ref[d, 0:8, LANES:] = small
        mine_ref[d, 8:16, LANES:] = jnp.zeros((8, CH), f32)
        theirs_ref[d, 0:8, LANES:] = small
        theirs_ref[d, 8:16, LANES:] = jnp.zeros((8, CH), f32)


def pair_kernel(mine_ref, got_ref, *outs):
    for d in range(4):
        outs[d][...] = mine_ref[d] + got_ref[d]


def row_kernel(shards, o0_ref, o1_ref, o2_ref, o3_ref, out_ref):
    total = (o0_ref[...] + o1_ref[...]) + (o2_ref[...] + o3_ref[...])
    share = LANES // shards
    small = total[0:8, LANES:]
    for k in range(shards):
        start = k * share
        base = start // CH * CH
        window = total[:, base : base + 2 * CH]
        if start > base:
            window = pltpu.roll(window, 2 * CH - (start - base), 1)
        out_ref[k, 0:16] = window[:, :CH]
        out_ref[k, 16:24] = small


def final_kernel(parts_ref, weight_ref, projection_ref, bias_ref):
    total = parts_ref[0]
    for k in range(1, parts_ref.shape[0]):
        total = total + parts_ref[k]
    weight_ref[...] = total[0:16, : weight_ref.shape[1]]
    projection_ref[...] = total[16 : 16 + L]
    bias_ref[...] = total[16 + L : 17 + L]


def on_device(frames, conv_weight, conv_bias, projection, levels, centres, code_grad):
    shards = lax.axis_size("tm")
    strips = lax.axis_size("space")
    both = ("tm", "space")
    shape = jax.ShapeDtypeStruct
    smem = pl.BlockSpec(memory_space=pltpu.SMEM)

    later = [(i, i + 1) for i in range(shards - 1)]
    lower = [(i, i + 1) for i in range(strips - 1)]
    upper = [(b, a) for a, b in lower]
    later_lower = [(a * strips + p, b * strips + q) for a, b in later for p, q in lower]
    later_upper = [(a * strips + p, b * strips + q) for a, b in later for p, q in upper]
    top, bottom = frames[:, 0], frames[:, 3]
    earlier = lax.ppermute(frames[2:], "tm", later)
    up = lax.ppermute(bottom, "space", lower)
    down = lax.ppermute(top, "space", upper)
    corner_up = lax.ppermute(bottom[2:], both, later_lower)
    corner_down = lax.ppermute(top[2:], both, later_upper)

    code_shape = (code_grad.shape[1], code_grad.shape[2], code_grad.shape[0])
    quantized, codes = call(
        code_kernel,
        [shape(code_shape, f32), shape((shards, CH), f32)],
        [smem] + vmem(2),
    )(levels, jnp.transpose(centres, (1, 2, 0)), jnp.transpose(code_grad, (1, 2, 0)))
    quantized = jnp.transpose(quantized, (2, 0, 1))
    codes = lax.all_to_all(codes.reshape(shards, 1, CH), "tm", 0, 0, tiled=True)
    codes = codes.reshape(shards, CH)

    total_cells = 4 * shards * 4 * strips * W
    mine, theirs = call(
        lambda *refs: block_kernel(total_cells, *refs),
        [shape((4, 16, WIDE), f32)] * 2,
        vmem(10),
        [
            pltpu.VMEM((6, 6, W, CH), bf16),
            pltpu.VMEM((9 * CH, 3 * CH), bf16),
            pltpu.VMEM((4, 4, W, CH), f32),
            pltpu.VMEM((3 * CH, 16 * W), bf16),
            pltpu.VMEM((3 * CH, 9 * CH), f32),
        ],
    )(
        frames,
        earlier,
        up,
        down,
        corner_up,
        corner_down,
        conv_weight,
        conv_bias.reshape(1, CH),
        projection.T,
        codes,
    )

    def swapped(value, step):
        return lax.ppermute(value, "space", [(i, i ^ step) for i in range(strips)])

    summed = call(pair_kernel, [shape((16, WIDE), f32)] * 4, vmem(2))(mine, swapped(theirs, 1))
    received = [summed[0]] + [swapped(summed[d], 2 * d) for d in range(1, 4)]
    (chunks,) = call(
        lambda *refs: row_kernel(shards, *refs), [shape((shards, 24, CH), f32)], vmem(4)
    )(*received)
    parts = lax.all_to_all(chunks, "tm", 0, 0, tiled=True)
    weight_grad, projection_grad, bias_grad = call(
        final_kernel,
        [shape((16, LANES // shards), f32), shape((L, CH), f32), shape((1, CH), f32)],
        vmem(1),
    )(parts)
    return quantized, weight_grad.T, projection_grad.T, bias_grad.reshape(CH)


def solution(mesh):
    return jax.shard_map(
        on_device,
        mesh=mesh,
        in_specs=(
            P("tm", "space", None, None),
            P(),
            P(),
            P(),
            P(),
            P(None, "space", "tm"),
            P(None, "space", "tm"),
        ),
        out_specs=(P(None, "space", "tm"), P("tm", "space"), P(), P()),
        check_vma=False,
    )
```

time: 317 us -> 85.9 us (0.27); the launches traced: 313 us -> 85.2 us
  blocking collectives: 177 us -> 36.4 us
  waiting for transfers between devices: 53 us -> 15.1 us
  matrix products: 21.1 us -> 0 us
  local copies, waits for them, and re-layouts: 20.7 us -> 4.02 us
  between operations: 15.1 us -> 0.79 us
  Pallas kernels: 0 us -> 9.34 us
  other arithmetic: 3.86 us -> 0 us
    unnamed x1 -> x0, blocking collectives: 84 us -> none
    psum x1 -> x0, blocking collectives: 77.5 us -> none  [on_device(): lax.psum((projection_part, bias_part), ('tm', 'space'))]
    unnamed x4 -> x0, waiting for transfers between devices: 33.1 us -> none
    all_to_all x1 -> x2, blocking collectives: 15.2 us -> 36.4 us  [the longest x1 19.1 us: on_device(): codes = lax.all_to_all(codes.reshape(shards, 1, CH), 'tm', 0, 0, tiled=True)]
    dot_general x21 -> x0, matrix products: 21.1 us -> none  [the longest x9 11.6 us: on_device(): lax.dot_general(tap_slab, low_grad, (((0,), (0,)), ((), ())), preferred_e...]
    ppermute x3 -> x9, starting transfers between devices: 5.99 us -> 19.6 us  [the longest x1 5.27 us: on_device(): corner_up = lax.ppermute(bottom[2:], both, later_lower)]
    all_to_all x1 -> x0, starting transfers between devices: 12.5 us -> none  [on_device(): lax.all_to_all(latent, 'tm', split_axis=2, concat_axis=0, tiled=True)]
    all_to_all x1 -> x0, waiting for transfers between devices: 10.5 us -> none  [on_device(): lax.all_to_all(latent, 'tm', split_axis=2, concat_axis=0, tiled=True)]
  transfers between devices with their start and end apart: 7 -> 9, of which waited for: 4 -> 4; matrix products, arithmetic and copies ran while one was open for 1% -> 0% of each run, Pallas kernels for 0% -> 1%
where the time goes in v1:
time: 85.9 us; the launch traced here: 85.2 us
  blocking collectives  36.4 us (42%)
  starting transfers between devices  19.6 us (23%)
  waiting for transfers between devices  15.1 us (18%)
  Pallas kernels  9.34 us (11%)
  local copies, waits for them, and re-layouts  4.02 us (5%)
    all_to_all x1, blocking collectives, on_device(): codes = lax.all_to_all(codes.reshape(shards, 1, CH), 'tm', 0, 0, tiled=True)  19.1 us
    all_to_all x1, blocking collectives, on_device(): parts = lax.all_to_all(chunks, 'tm', 0, 0, tiled=True)  17.3 us
    ppermute x4, waiting for transfers between devices, swapped(): return lax.ppermute(value, 'space', [(i, i ^ step) for i in range(strips)])  15.1 us
    pallas_call x1, Pallas kernels, on_device(): call(lambda *refs: block_kernel(total_cells, *refs), [shape((4, 16, WIDE)...  7.2 us
    ppermute x1, starting transfers between devices, on_device(): corner_up = lax.ppermute(bottom[2:], both, later_lower)  5.27 us
    ppermute x4, starting transfers between devices, swapped(): return lax.ppermute(value, 'space', [(i, i ^ step) for i in range(strips)])  5.26 us
    ppermute x1, starting transfers between devices, on_device(): earlier = lax.ppermute(frames[2:], 'tm', later)  3.4 us
    ppermute x1, starting transfers between devices, on_device(): up = lax.ppermute(bottom, 'space', lower)  3.04 us
  transfers between devices with their start and end apart: 9, of which 4 were waited for; matrix products, arithmetic and copies ran while one was open for 0% of the time, Pallas kernels for 1%

profile of v1, /device:TPU:2, one launch (start us, length us, event | category | flops | bytes accessed | tf_op | source)
XLA Modules:
  0.0 85.2 jit_solution(2912969010203340962)
XLA Ops:
  0.6 0.0 copy-start
  0.6 0.0 copy-start.1
  0.7 1.1 %slice_bitcast_fusion = (bf16[4,128,128]{2,1,0:T(8,128)(2,1)S(1)}, bf16[4,128,128]{2,1,0:T(8,128)(2,1)S(1)}) fusion(bf16[4,4,128,128]{3,2,1,0:T(8,128)(2,1)} %refs_0_.1), kind=kLoop, calls=%fused_computation | loop fusion | bytes 524288 | tf_op jit(solution)/shard_map/squeeze | solution.py:246
  1.8 1.3 %collective-permute-start.2 = (bf16[4,128,128]{2,1,0:T(8,128)(2,1)S(1)}, bf16[4,128,128]{2,1,0:T(8,128)(2,1)S(1)}, u32[]{:S(2)}, u32[]{:S(2)}) collective-permute-start(bf16[4,128,128]{2,1,0:T(8,128)(2,1)S(1)} %get-tuple-element.28), channel_id=1, source_target_pairs={{1,0},{2,1},{3,2},{4,3},{5,4},{6,5},{7,6},{9,8},{10,9},{11,10},{12... | collective-permute-start | bytes 393224 | tf_op jit(solution)/shard_map/ppermute | solution.py:249
  3.1 3.0 %collective-permute-start.1 = (bf16[4,128,128]{2,1,0:T(8,128)(2,1)S(1)}, bf16[4,128,128]{2,1,0:T(8,128)(2,1)S(1)}, u32[]{:S(2)}, u32[]{:S(2)}) collective-permute-start(bf16[4,128,128]{2,1,0:T(8,128)(2,1)S(1)} %get-tuple-element.29), channel_id=1, source_target_pairs={{0,1},{1,2},{2,3},{3,4},{4,5},{5,6},{6,7},{8,9},{9,10},{10,11},{11... | collective-permute-start | bytes 393224 | tf_op jit(solution)/shard_map/ppermute | solution.py:248
  6.1 0.0 copy-done
  6.1 3.4 %collective-permute-start = (bf16[2,4,128,128]{3,2,1,0:T(8,128)(2,1)S(1)}, bf16[2,4,128,128]{3,2,1,0:T(8,128)(2,1)S(1)}, u32[]{:S(2)}, u32[]{:S(2)}) collective-permute-start(bf16[2,4,128,128]{3,2,1,0:T(8,128)(2,1)S(1)} %slice.23), channel_id=1, source_target_pairs={{0,8},{8,16},{16,24},{24,32},{32,40},{40,48},{48,56},{56,64},{64,7... | collective-permute-start | bytes 786440 | tf_op jit(solution)/shard_map/ppermute | solution.py:247
  9.6 1.3 %collective-permute-start.4 = (bf16[2,128,128]{2,1,0:T(8,128)(2,1)S(1)}, bf16[2,128,128]{2,1,0:T(8,128)(2,1)S(1)}, u32[]{:S(2)}, u32[]{:S(2)}) collective-permute-start(bf16[2,128,128]{2,1,0:T(8,128)(2,1)S(1)} %get-tuple-element.26), channel_id=1, source_target_pairs={{1,8},{2,9},{3,10},{4,11},{5,12},{6,13},{7,14},{9,16},{10,17},{11,... | collective-permute-start | bytes 196616 | tf_op jit(solution)/shard_map/ppermute | solution.py:251
  10.9 5.3 %collective-permute-start.3 = (bf16[2,128,128]{2,1,0:T(8,128)(2,1)S(1)}, bf16[2,128,128]{2,1,0:T(8,128)(2,1)S(1)}, u32[]{:S(2)}, u32[]{:S(2)}) collective-permute-start(bf16[2,128,128]{2,1,0:T(8,128)(2,1)S(1)} %get-tuple-element.27), channel_id=1, source_target_pairs={{0,9},{1,10},{2,11},{3,12},{4,13},{5,14},{6,15},{8,17},{9,18},{10,... | collective-permute-start | bytes 196616 | tf_op jit(solution)/shard_map/ppermute | solution.py:250
  16.1 0.0 copy-start.2
  16.2 0.8 copy-done.2
  16.9 0.0 copy-start.3
  16.9 0.8 copy-done.3
  17.7 0.0 copy-start.5
  17.7 0.7 copy-done.5
  18.4 1.2 %shard_map.102 = (f32[4,24,32]{2,1,0:T(8,128)}, f32[32,128]{1,0:T(8,128)S(1)}) custom-call(s32[6]{0:T(128)S(1)} %copy-done.5, s32[4,24,32]{2,1,0:T(8,128)S(1)} %bitcast.29, f32[4,24,32]{2,1,0:T(8,128)S(1)} %bitcast.30), custom_call_target="tpu_custom_call" | custom-call | tf_op jit(solution)/shard_map/pallas_call | solution.py:254
  19.6 19.1 %all_to_all.10 = f32[32,1,128]{2,1,0:T(1,128)S(1)} all-to-all(f32[32,1,128]{2,1,0:T(1,128)S(1)} %bitcast.31), channel_id=1, replica_groups=mesh['tm'=32,'space'=8] {'tm'}, dimensions={0} | all-to-all | bytes 32768 | tf_op jit(solution)/shard_map/all_to_all | solution.py:260
  38.6 0.0 copy-start.4
  38.6 0.0 collective-permute-done.4.refs_5_
  38.6 0.0 collective-permute-done.3.refs_4_
  38.6 0.0 collective-permute-done.2.refs_3_
  38.7 0.0 collective-permute-done.1.refs_2_
  38.7 0.0 collective-permute-done.refs_1_
  38.7 0.0 copy-start.6
  38.7 0.0 copy-done.1
  38.7 0.6 copy-done.4
  39.3 0.0 copy-done.6
  39.3 7.2 %shard_map.103 = (f32[4,16,3584]{2,1,0:T(8,128)S(1)}, f32[4,16,3584]{2,1,0:T(8,128)S(1)}) custom-call(bf16[4,4,128,128]{3,2,1,0:T(8,128)(2,1)S(1)} %copy-done, bf16[2,4,128,128]{3,2,1,0:T(8,128)(2,1)S(1)} %collective-permute-done.refs_1_, bf16[4,128,128]{2,1,0:T(8,128)(2,1)S(1)} %collective-permute-done.1.refs_2_, ...), custom_call_target="tpu_custom_call" | custom-call | tf_op jit(solution)/shard_map/pallas_call | solution.py:264
  46.5 0.5 collective-permute-start.5
  47.0 2.1 %collective-permute-done.5.got_ref = f32[4,16,3584]{2,1,0:T(8,128)S(1)} collective-permute-done((f32[4,16,3584]{2,1,0:T(8,128)S(1)}, f32[4,16,3584]{2,1,0:T(8,128)S(1)}, u32[]{:S(2)}, u32[]{:S(2)}) %collective-permute-start.5) | collective-permute-done | bytes 917536 | tf_op jit(solution)/shard_map/ppermute | solution.py:289
  49.1 0.1 shard_map.104
  49.2 1.7 %collective-permute-start.6 = (f32[16,3584]{1,0:T(8,128)S(1)}, f32[16,3584]{1,0:T(8,128)S(1)}, u32[]{:S(2)}, u32[]{:S(2)}) collective-permute-start(f32[16,3584]{1,0:T(8,128)S(1)} %get-tuple-element.20), channel_id=1, source_target_pairs={{0,2},{1,3},{2,0},{3,1},{4,6},{5,7},{6,4},{7,5},{8,10},{9,11},{10,... | collective-permute-start | bytes 688136 | tf_op jit(solution)/shard_map/ppermute | solution.py:289
  50.9 2.9 %collective-permute-start.7 = (f32[16,3584]{1,0:T(8,128)S(1)}, f32[16,3584]{1,0:T(8,128)S(1)}, u32[]{:S(2)}, u32[]{:S(2)}) collective-permute-start(f32[16,3584]{1,0:T(8,128)S(1)} %get-tuple-element.21), channel_id=1, source_target_pairs={{0,4},{1,5},{2,6},{3,7},{4,0},{5,1},{6,2},{7,3},{8,12},{9,13},{10,... | collective-permute-start | bytes 688136 | tf_op jit(solution)/shard_map/ppermute | solution.py:289
  53.8 0.2 collective-permute-start.8
  54.0 3.7 %collective-permute-done.6.refs_1_ = f32[16,3584]{1,0:T(8,128)S(1)} collective-permute-done((f32[16,3584]{1,0:T(8,128)S(1)}, f32[16,3584]{1,0:T(8,128)S(1)}, u32[]{:S(2)}, u32[]{:S(2)}) %collective-permute-start.6) | collective-permute-done | bytes 229408 | tf_op jit(solution)/shard_map/ppermute | solution.py:289
  57.8 6.7 %collective-permute-done.7.refs_2_ = f32[16,3584]{1,0:T(8,128)S(1)} collective-permute-done((f32[16,3584]{1,0:T(8,128)S(1)}, f32[16,3584]{1,0:T(8,128)S(1)}, u32[]{:S(2)}, u32[]{:S(2)}) %collective-permute-start.7) | collective-permute-done | bytes 229408 | tf_op jit(solution)/shard_map/ppermute | solution.py:289
  64.4 2.6 %collective-permute-done.8.refs_3_ = f32[16,3584]{1,0:T(8,128)S(1)} collective-permute-done((f32[16,3584]{1,0:T(8,128)S(1)}, f32[16,3584]{1,0:T(8,128)S(1)}, u32[]{:S(2)}, u32[]{:S(2)}) %collective-permute-start.8) | collective-permute-done | bytes 229408 | tf_op jit(solution)/shard_map/ppermute | solution.py:289
  67.0 0.2 shard_map.105
  67.2 17.3 %all_to_all.11.parts_ref = f32[32,24,128]{2,1,0:T(8,128)S(1)} all-to-all(f32[32,24,128]{2,1,0:T(8,128)S(1)} %shard_map.105), channel_id=1, replica_groups=mesh['tm'=32,'space'=8] {'tm'}, dimensions={0} | all-to-all | bytes 786432 | tf_op jit(solution)/shard_map/all_to_all | solution.py:296
  84.5 0.6 shard_map.106
  (2 shorter events, 0.0 us)
Async XLA Ops:
  0.6 5.5 %copy-start = (bf16[4,4,128,128]{3,2,1,0:T(8,128)(2,1)S(1)}, bf16[4,4,128,128]{3,2,1,0:T(8,128)(2,1)}, u32[]{:S(2)}) copy-start(bf16[4,4,128,128]{3,2,1,0:T(8,128)(2,1)} %refs_0_.1) | copy-start | bytes 1572868
  0.6 38.1 %copy-start.1 = (bf16[3456,128]{1,0:T(8,128)(2,1)S(1)}, bf16[3456,128]{1,0:T(8,128)(2,1)}, u32[]{:S(2)}) copy-start(bf16[3456,128]{1,0:T(8,128)(2,1)} %refs_6_.1) | copy-start | bytes 2654212
  1.8 36.9 %collective-permute-start.2 = (bf16[4,128,128]{2,1,0:T(8,128)(2,1)S(1)}, bf16[4,128,128]{2,1,0:T(8,128)(2,1)S(1)}, u32[]{:S(2)}, u32[]{:S(2)}) collective-permute-start(bf16[4,128,128]{2,1,0:T(8,128)(2,1)S(1)} %get-tuple-element.28), channel_id=1, source_target_pairs={{1,0},{2,1},{3,2},{4,3},{5,4},{6,5},{7,6},{9,8},{10,9},{11,10},{12... | collective-permute-start | bytes 393224 | tf_op jit(solution)/shard_map/ppermute | solution.py:249
  3.1 35.6 %collective-permute-start.1 = (bf16[4,128,128]{2,1,0:T(8,128)(2,1)S(1)}, bf16[4,128,128]{2,1,0:T(8,128)(2,1)S(1)}, u32[]{:S(2)}, u32[]{:S(2)}) collective-permute-start(bf16[4,128,128]{2,1,0:T(8,128)(2,1)S(1)} %get-tuple-element.29), channel_id=1, source_target_pairs={{0,1},{1,2},{2,3},{3,4},{4,5},{5,6},{6,7},{8,9},{9,10},{10,11},{11... | collective-permute-start | bytes 393224 | tf_op jit(solution)/shard_map/ppermute | solution.py:248
  6.1 32.5 %collective-permute-start = (bf16[2,4,128,128]{3,2,1,0:T(8,128)(2,1)S(1)}, bf16[2,4,128,128]{3,2,1,0:T(8,128)(2,1)S(1)}, u32[]{:S(2)}, u32[]{:S(2)}) collective-permute-start(bf16[2,4,128,128]{3,2,1,0:T(8,128)(2,1)S(1)} %slice.23), channel_id=1, source_target_pairs={{0,8},{8,16},{16,24},{24,32},{32,40},{40,48},{48,56},{56,64},{64,7... | collective-permute-start | bytes 786440 | tf_op jit(solution)/shard_map/ppermute | solution.py:247
  9.6 29.1 %collective-permute-start.4 = (bf16[2,128,128]{2,1,0:T(8,128)(2,1)S(1)}, bf16[2,128,128]{2,1,0:T(8,128)(2,1)S(1)}, u32[]{:S(2)}, u32[]{:S(2)}) collective-permute-start(bf16[2,128,128]{2,1,0:T(8,128)(2,1)S(1)} %get-tuple-element.26), channel_id=1, source_target_pairs={{1,8},{2,9},{3,10},{4,11},{5,12},{6,13},{7,14},{9,16},{10,17},{11,... | collective-permute-start | bytes 196616 | tf_op jit(solution)/shard_map/ppermute | solution.py:251
  10.9 27.8 %collective-permute-start.3 = (bf16[2,128,128]{2,1,0:T(8,128)(2,1)S(1)}, bf16[2,128,128]{2,1,0:T(8,128)(2,1)S(1)}, u32[]{:S(2)}, u32[]{:S(2)}) collective-permute-start(bf16[2,128,128]{2,1,0:T(8,128)(2,1)S(1)} %get-tuple-element.27), channel_id=1, source_target_pairs={{0,9},{1,10},{2,11},{3,12},{4,13},{5,14},{6,15},{8,17},{9,18},{10,... | collective-permute-start | bytes 196616 | tf_op jit(solution)/shard_map/ppermute | solution.py:250
  16.1 0.8 copy-start.2
  16.9 0.8 copy-start.3
  17.7 0.7 copy-start.5
  38.6 0.7 copy-start.4
  38.7 0.7 copy-start.6
  46.5 2.6 %collective-permute-start.5 = (f32[4,16,3584]{2,1,0:T(8,128)S(1)}, f32[4,16,3584]{2,1,0:T(8,128)S(1)}, u32[]{:S(2)}, u32[]{:S(2)}) collective-permute-start(f32[4,16,3584]{2,1,0:T(8,128)S(1)} %get-tuple-element.18), channel_id=1, source_target_pairs={{0,1},{1,0},{2,3},{3,2},{4,5},{5,4},{6,7},{7,6},{8,9},{9,8},{10,11... | collective-permute-start | bytes 2752520 | tf_op jit(solution)/shard_map/ppermute | solution.py:289
  49.2 8.5 %collective-permute-start.6 = (f32[16,3584]{1,0:T(8,128)S(1)}, f32[16,3584]{1,0:T(8,128)S(1)}, u32[]{:S(2)}, u32[]{:S(2)}) collective-permute-start(f32[16,3584]{1,0:T(8,128)S(1)} %get-tuple-element.20), channel_id=1, source_target_pairs={{0,2},{1,3},{2,0},{3,1},{4,6},{5,7},{6,4},{7,5},{8,10},{9,11},{10,... | collective-permute-start | bytes 688136 | tf_op jit(solution)/shard_map/ppermute | solution.py:289
  50.9 13.5 %collective-permute-start.7 = (f32[16,3584]{1,0:T(8,128)S(1)}, f32[16,3584]{1,0:T(8,128)S(1)}, u32[]{:S(2)}, u32[]{:S(2)}) collective-permute-start(f32[16,3584]{1,0:T(8,128)S(1)} %get-tuple-element.21), channel_id=1, source_target_pairs={{0,4},{1,5},{2,6},{3,7},{4,0},{5,1},{6,2},{7,3},{8,12},{9,13},{10,... | collective-permute-start | bytes 688136 | tf_op jit(solution)/shard_map/ppermute | solution.py:289
  53.8 13.2 %collective-permute-start.8 = (f32[16,3584]{1,0:T(8,128)S(1)}, f32[16,3584]{1,0:T(8,128)S(1)}, u32[]{:S(2)}, u32[]{:S(2)}) collective-permute-start(f32[16,3584]{1,0:T(8,128)S(1)} %get-tuple-element.22), channel_id=1, source_target_pairs={{0,6},{1,7},{2,4},{3,5},{4,2},{5,3},{6,0},{7,1},{8,14},{9,15},{10,... | collective-permute-start | bytes 688136 | tf_op jit(solution)/shard_map/ppermute | solution.py:289

commit v2 on v1

v2 whole, which is shorter than its diff:
```python
import jax
import jax.numpy as jnp
from jax import lax
from jax.experimental import pallas as pl
from jax.experimental.pallas import tpu as pltpu
from jax.sharding import PartitionSpec as P

offset_scale = 0.45
commit_weight = 0.25
highest = lax.Precision.HIGHEST
bf16 = jnp.bfloat16
f32 = jnp.float32
MIB = 1024 * 1024
CH = 128
L = 6
W = 128
TAPS = 27
LANES = TAPS * CH
WIDE = LANES + CH
STATE = 16 * W
SMALL = 20 * W


VMEM = pl.BlockSpec(memory_space=pltpu.VMEM)
ANY = pl.BlockSpec(memory_space=pl.ANY)


def call(kernel, out_shape, in_specs, scratch=(), aliases=None):
    return pl.pallas_call(
        kernel,
        out_shape=out_shape,
        in_specs=in_specs,
        out_specs=[VMEM] * len(out_shape),
        scratch_shapes=list(scratch),
        input_output_aliases=aliases or {},
        compiler_params=pltpu.CompilerParams(vmem_limit_bytes=24 * MIB),
    )


def copy_all(pairs, sems):
    copies = [pltpu.make_async_copy(src, dst, sems.at[i]) for i, (src, dst) in enumerate(pairs)]
    for copy in copies:
        copy.start()
    for copy in copies:
        copy.wait()


def half_ranges(levels_ref, channel):
    half = jnp.ones(channel.shape, f32)
    for j in range(L):
        half = jnp.where(channel == j, (levels_ref[j].astype(f32) - 1.0) * 0.5, half)
    return half


def code_kernel(grad_ref, codes_ref):
    rows, columns, frames = grad_ref.shape
    stacked = jnp.concatenate([grad_ref[h] for h in range(rows)], 0)
    padded = jnp.pad(stacked, ((0, CH - rows * columns), (0, CH - frames)))
    codes_ref[...] = padded.T[:frames]


def edge_kernel(frames_any, x_ref, top_ref, bottom_ref, sems):
    copy_all(
        [
            (frames_any, x_ref.at[:, 1:5]),
            (frames_any.at[:, 0], top_ref),
            (frames_any.at[:, 3], bottom_ref),
        ],
        sems,
    )


def late_kernel(own_ref, up_ref, down_ref, x_ref, late_ref):
    for t in range(4):
        x_ref[t, 0] = up_ref[t]
        x_ref[t, 5] = down_ref[t]
    for t in range(2):
        late_ref[t, 0] = up_ref[t + 2]
        late_ref[t, 5] = down_ref[t + 2]
        for h in range(1, 5):
            late_ref[t, h] = own_ref[t + 2, h]


def block_of(early_ref, x_ref):
    return lambda t, h: early_ref[t, h] if t < 2 else x_ref[t - 2, h]


def shifted_rows(value, step):
    row = lax.broadcasted_iota(jnp.int32, value.shape, 0)
    rolled = pltpu.roll(value, step % value.shape[0], 0)
    edge = 0 if step == 1 else value.shape[0] - 1
    return jnp.where(row == edge, 0.0, rolled)


def shifted_lanes(value, step):
    lane = lax.broadcasted_iota(jnp.int32, value.shape, 1)
    rolled = pltpu.roll(value, step % value.shape[1], 1)
    edge = 0 if step == 1 else value.shape[1] - 1
    return jnp.where(lane == edge, 0.0, rolled)


def forward_kernel(
    levels_any,
    centres_any,
    earlier_ref,
    x_ref,
    weight_any,
    bias_any,
    projection_any,
    early_ref,
    state_ref,
    quantized_ref,
    wide_ref,
    levels_ref,
    centres_ref,
    bias_ref,
    projection_ref,
    sems,
):
    first = (lax.axis_index("z") == 0) & (lax.axis_index("x") == 0)
    copy_all(
        [
            (weight_any.at[:, 0], wide_ref.at[:, :, 0:CH]),
            (weight_any.at[:, 1], wide_ref.at[:, :, CH : 2 * CH]),
            (weight_any.at[:, 2], wide_ref.at[:, :, 2 * CH : 3 * CH]),
            (levels_any, levels_ref),
            (centres_any, centres_ref),
            (bias_any, bias_ref),
            (projection_any, projection_ref.at[0:L]),
        ],
        sems,
    )
    projection_ref[L:8] = jnp.zeros((8 - L, CH), f32)
    rows, columns, groups = centres_ref.shape
    channel = lax.broadcasted_iota(jnp.int32, (columns, groups), 0) % L
    half = half_ranges(levels_ref, channel)
    for h in range(rows):
        quantized_ref[h] = (centres_ref[h].astype(f32) - half) / half

    @pl.when(first)
    def _():
        for t in range(2):
            early_ref[t] = x_ref[0]

    @pl.when(jnp.logical_not(first))
    def _():
        early_ref[...] = earlier_ref[...]

    block = block_of(early_ref, x_ref)

    wide = wide_ref[...].reshape(9 * CH, 3 * CH)
    bias = bias_ref[...]
    pooled = [jnp.zeros((W, CH), f32) for _ in range(4)]
    for t in range(4):
        for h in range(4):
            left = jnp.concatenate([block(t + a, h + b) for a in range(3) for b in range(3)], 1)
            z = jnp.dot(left, wide, preferred_element_type=f32)
            preact = (
                bias
                + shifted_rows(z[:, :CH], 1)
                + z[:, CH : 2 * CH]
                + shifted_rows(z[:, 2 * CH :], -1)
            )
            sigmoid = 1.0 / (1.0 + jnp.exp(-preact))
            place = (t * 4 + h) * W
            state_ref[place : place + W] = sigmoid * (1.0 + preact * (1.0 - sigmoid))
            pooled[h] = pooled[h] + (preact * sigmoid).astype(bf16).astype(f32)
    pooled = jnp.concatenate(pooled, 0) * 0.25
    state_ref[STATE : STATE + 4 * W] = pooled
    projection = projection_ref[...]
    latent = lax.dot_general(
        projection, pooled, (((1,), (1,)), ((), ())), precision=highest, preferred_element_type=f32
    )
    squashed = jnp.tanh(latent)
    for h in range(4):
        state_ref[SMALL + 8 * h : SMALL + 8 * h + 8] = squashed[:, h * W : (h + 1) * W]
    state_ref[SMALL + 32 : SMALL + 40] = projection
    channel = lax.broadcasted_iota(jnp.int32, (8, CH), 0)
    state_ref[SMALL + 40 : SMALL + 48] = half_ranges(levels_ref, channel)


def window(early_ref, x_ref, a, b):
    blocks = []
    if a < 2:
        blocks.append(early_ref[a:2, b : b + 4].reshape((2 - a) * 4 * W, CH))
    if a > 0:
        blocks.append(x_ref[max(a - 2, 0) : a + 2, b : b + 4].reshape(-1, CH))
    else:
        blocks.append(x_ref[0:2, b : b + 4].reshape(8 * W, CH))
    return jnp.concatenate(blocks, 0) if len(blocks) > 1 else blocks[0]


def backward_kernel(
    total_cells,
    early_ref,
    x_ref,
    state_ref,
    code_ref,
    mine_ref,
    theirs_ref,
    low_ref,
    grad_ref,
):
    core = lax.axis_index("c")
    pooled = state_ref[STATE : STATE + 4 * W]
    squashed = jnp.concatenate(
        [state_ref[SMALL + 8 * h : SMALL + 8 * h + 8] for h in range(4)], 1
    )
    projection = state_ref[SMALL + 32 : SMALL + 40]
    half = state_ref[SMALL + 40 : SMALL + 48]
    tile_of = lax.broadcasted_iota(jnp.int32, (W, 32), 1)
    column = lax.broadcasted_iota(jnp.int32, (W, 32), 0)
    spread = jnp.where(column // 4 == tile_of, 1.0, 0.0).astype(f32)
    repeated = jnp.dot(spread, code_ref[...], precision=highest, preferred_element_type=f32)
    place = lax.broadcasted_iota(jnp.int32, (W, CH), 1)
    column = lax.broadcasted_iota(jnp.int32, (W, CH), 0)
    repeated = jnp.where((place % 24) // L == column % 4, repeated, 0.0)
    wanted = lax.broadcasted_iota(jnp.int32, (32, CH), 0)
    place = lax.broadcasted_iota(jnp.int32, (32, CH), 1)
    pick = jnp.where((place // 24 == wanted // 8) & (place % L == wanted % 8), 1.0, 0.0).astype(f32)
    codes = lax.dot_general(
        pick, repeated, (((1,), (1,)), ((), ())), precision=highest, preferred_element_type=f32
    )
    codes = jnp.concatenate([codes[8 * h : 8 * h + 8] / half for h in range(4)], 1)
    code_step = (
        (codes + 2.0 * commit_weight * offset_scale * squashed)
        * offset_scale
        * (1.0 - squashed * squashed)
        * float(total_cells) ** (-0.5)
    )
    projection_part = jnp.dot(code_step, pooled, precision=highest, preferred_element_type=f32)
    pooled_grad = 0.25 * lax.dot_general(
        code_step, projection, (((0,), (0,)), ((), ())), precision=highest, preferred_element_type=f32
    )
    bias_part = jnp.zeros((8, CH), f32)
    for t in range(4):
        for h in range(4):
            place = (t * 4 + h) * W
            pre_grad = pooled_grad[h * W : (h + 1) * W] * state_ref[place : place + W]
            bias_part = bias_part + pre_grad.reshape(W // 8, 8, CH).sum(0)
            turned = pre_grad.T
            low_ref[0:CH, place : place + W] = shifted_lanes(turned, -1).astype(bf16)
            low_ref[CH : 2 * CH, place : place + W] = turned.astype(bf16)
            low_ref[2 * CH :, place : place + W] = shifted_lanes(turned, 1).astype(bf16)
    bias_row = bias_part.sum(0, keepdims=True)
    row = lax.broadcasted_iota(jnp.int32, (8, CH), 0)
    small = jnp.where(row == L, bias_row, projection_part)
    taps = [(a, b) for a in range(3) for b in range(3)]
    for start in range(0, 9, 2):
        group = taps[start : start + 2]
        right = jnp.concatenate([window(early_ref, x_ref, a, b) for a, b in group], 1)
        grad_ref[:, start * CH : (start + len(group)) * CH] = jnp.dot(
            low_ref[...], right, preferred_element_type=f32
        )
    for y in range(4):
        for c in range(3):
            own = pl.multiple_of(c * CH + 32 * y + 16 * core, 16)
            other = pl.multiple_of(c * CH + 32 * y + 16 * (1 - core), 16)
            for tap in range(9):
                to = slice((3 * tap + c) * CH, (3 * tap + c + 1) * CH)
                mine_ref[y, :, to] = grad_ref[pl.ds(own, 16), tap * CH : (tap + 1) * CH]
                theirs_ref[y, :, to] = grad_ref[pl.ds(other, 16), tap * CH : (tap + 1) * CH]
        mine_ref[y, 0:8, LANES:] = small
        mine_ref[y, 8:16, LANES:] = jnp.zeros((8, CH), f32)
        theirs_ref[y, 0:8, LANES:] = small
        theirs_ref[y, 8:16, LANES:] = jnp.zeros((8, CH), f32)


def pair_kernel(mine_ref, got_ref, out_ref):
    small = mine_ref[0, 0:8, LANES:] + got_ref[0, 0:8, LANES:]
    high = small.astype(bf16).astype(f32)
    small = jnp.concatenate([high, small - high], 0).astype(bf16)
    share = LANES // 32
    for y in range(4):
        for k in range(32):
            start = k * share
            base = start // CH * CH
            window = mine_ref[y, :, base : base + 2 * CH] + got_ref[y, :, base : base + 2 * CH]
            if start > base:
                window = pltpu.roll(window, 2 * CH - (start - base), 1)
            z, x = divmod(k, 4)
            out_ref[x * 4 + y, z * 16 : (z + 1) * 16] = window[:, :CH].astype(bf16)
        for x in range(4):
            out_ref[x * 4 + y, 128:144] = small


def plane_kernel(parts_ref, out_ref):
    total = parts_ref[0].astype(f32)
    for k in range(1, parts_ref.shape[0]):
        total = total + parts_ref[k].astype(f32)
    small = total[128:136] + total[136:144]
    for z in range(8):
        out_ref[z, 0:16] = total[z * 16 : (z + 1) * 16]
        out_ref[z, 16:24] = small


def final_kernel(parts_ref, weight_ref, projection_ref, bias_ref):
    total = parts_ref[0]
    for k in range(1, parts_ref.shape[0]):
        total = total + parts_ref[k]
    weight_ref[...] = total[0:16, : weight_ref.shape[1]]
    projection_ref[...] = total[16 : 16 + L]
    bias_ref[...] = total[16 + L : 17 + L]


def on_device(frames, conv_weight, conv_bias, projection, levels, centres, code_grad):
    time_axes, row_axes, all_axes = ("z", "x"), ("y", "c"), ("z", "x", "y", "c")
    shards = 32
    strips = 8
    shape = jax.ShapeDtypeStruct
    dma = pltpu.SemaphoreType.DMA

    code_grad = jnp.transpose(code_grad, (1, 2, 0))
    centres = jnp.transpose(centres, (1, 2, 0))
    lower = [(i, i + 1) for i in range(strips - 1)]
    edge = shape((4, W, CH), bf16)
    own = shape((4, 6, W, CH), bf16)
    x, top, bottom = call(edge_kernel, [own, edge, edge], [ANY], [dma((3,))])(frames)
    up = lax.ppermute(bottom, row_axes, lower)
    down = lax.ppermute(top, row_axes, [(b, a) for a, b in lower])
    (codes,) = call(code_kernel, [shape((shards, CH), f32)], [VMEM])(code_grad)
    codes = lax.all_to_all(codes.reshape(shards, 1, CH), time_axes, 0, 0, tiled=True)
    codes = codes.reshape(shards, CH)
    x, late = call(
        late_kernel, [own, shape((2, 6, W, CH), bf16)], [VMEM] * 3, aliases={0: 0}
    )(x, up, down)
    earlier = lax.ppermute(late, time_axes, [(i, i + 1) for i in range(shards - 1)])
    early, state, quantized = call(
        forward_kernel,
        [shape((2, 6, W, CH), bf16), shape((SMALL + 48, CH), f32), shape(centres.shape, f32)],
        [ANY] * 2 + [VMEM] * 2 + [ANY] * 3,
        [
            pltpu.VMEM((9, CH, 3 * CH), bf16),
            pltpu.SMEM((L,), jnp.int32),
            pltpu.VMEM(centres.shape, jnp.int32),
            pltpu.VMEM((1, CH), f32),
            pltpu.VMEM((8, CH), f32),
            dma((7,)),
        ],
    )(
        levels,
        centres,
        earlier,
        x,
        conv_weight.reshape(9, 3, CH, CH),
        conv_bias.reshape(1, CH),
        projection.T,
    )

    total_cells = 4 * shards * 4 * strips * W
    mine, theirs = call(
        lambda *refs: backward_kernel(total_cells, *refs),
        [shape((4, 16, WIDE), f32)] * 2,
        [VMEM] * 4,
        [pltpu.VMEM((3 * CH, 16 * W), bf16), pltpu.VMEM((3 * CH, 9 * CH), f32)],
    )(early, x, state, codes)

    got = lax.ppermute(theirs, "c", [(0, 1), (1, 0)])
    (chunks,) = call(pair_kernel, [shape((16, 144, CH), bf16)], [VMEM] * 2)(mine, got)
    chunks = lax.all_to_all(chunks, ("x", "y"), 0, 0, tiled=True)
    (chunks,) = call(plane_kernel, [shape((8, 24, CH), f32)], [VMEM])(chunks)
    parts = lax.all_to_all(chunks, "z", 0, 0, tiled=True)
    weight_grad, projection_grad, bias_grad = call(
        final_kernel,
        [shape((16, LANES // shards), f32), shape((L, CH), f32), shape((1, CH), f32)],
        [VMEM],
    )(parts)
    quantized = jnp.transpose(quantized, (2, 0, 1))
    return quantized, weight_grad.T, projection_grad.T, bias_grad.reshape(CH)


def solution(mesh):
    mesh = jax.sharding.Mesh(mesh.devices.reshape(8, 4, 4, 2), ("z", "x", "y", "c"))
    time, rows = ("z", "x"), ("y", "c")
    return jax.shard_map(
        on_device,
        mesh=mesh,
        in_specs=(
            P(time, rows, None, None),
            P(),
            P(),
            P(),
            P(),
            P(None, rows, time),
            P(None, rows, time),
        ),
        out_specs=(P(None, rows, time), P(time, rows), P(), P()),
        check_vma=False,
    )
```

time: 85.9 us -> 74.5 us (0.87)
  waiting for transfers between devices: 15.1 us -> 8.08 us
  blocking collectives: 36.4 us -> 32.3 us
  local copies, waits for them, and re-layouts: 4.02 us -> 2.78 us
  Pallas kernels: 9.34 us -> 10.4 us
    all_to_all x0 -> x1, starting transfers between devices: none -> 11.3 us  [on_device(): lax.all_to_all(codes.reshape(shards, 1, CH), time_axes, 0, 0, tiled=True)]
    ppermute x9 -> x4, starting transfers between devices: 19.6 us -> 8.54 us  [the longest x1 3.4 us: on_device(): lax.ppermute(late, time_axes, [(i, i + 1) for i in range(shards - 1)])]
    ppermute x9 -> x4, waiting for transfers between devices: 15.1 us -> 5.39 us  [the longest x1 3.29 us: on_device(): down = lax.ppermute(top, row_axes, [(b, a) for a, b in lower])]
    all_to_all x2, blocking collectives: 36.4 us -> 32.3 us  [the longest x1 17.9 us: on_device(): chunks = lax.all_to_all(chunks, ('x', 'y'), 0, 0, tiled=True)]
    all_to_all x0 -> x1, waiting for transfers between devices: none -> 2.69 us  [on_device(): lax.all_to_all(codes.reshape(shards, 1, CH), time_axes, 0, 0, tiled=True)]
    squeeze x1 -> x0, local copies, waits for them, and re-layouts: 1.1 us -> none  [on_device(): top, bottom = (frames[:, 0], frames[:, 3])]
    pallas_call x4 -> x7, Pallas kernels: 8.7 us -> 9.75 us  [the longest x1 4.39 us: on_device(): call(lambda *refs: backward_kernel(total_cells, *refs), [shape((4, 16, WI...]
    unnamed x14 -> x18, local copies, waits for them, and re-layouts: 2.9 us -> 2.78 us
  transfers between devices with their start and end apart: 9 -> 5, of which waited for: 4 -> 3; matrix products, arithmetic and copies ran while one was open for 0% -> 0% of each run, Pallas kernels for 1% -> 6%
where the time goes in v2:
time: 74.5 us; the launch traced here: 74.1 us
  blocking collectives  32.3 us (43%)
  starting transfers between devices  19.9 us (27%)
  Pallas kernels  10.4 us (14%)
  waiting for transfers between devices  8.08 us (11%)
  local copies, waits for them, and re-layouts  2.78 us (4%)
  between operations  0.78 us (1%)
    all_to_all x1, blocking collectives, on_device(): chunks = lax.all_to_all(chunks, ('x', 'y'), 0, 0, tiled=True)  17.9 us
    all_to_all x1, blocking collectives, on_device(): parts = lax.all_to_all(chunks, 'z', 0, 0, tiled=True)  14.4 us
    all_to_all x1, starting transfers between devices, on_device(): lax.all_to_all(codes.reshape(shards, 1, CH), time_axes, 0, 0, tiled=True)  11.3 us
    pallas_call x1, Pallas kernels, on_device(): call(lambda *refs: backward_kernel(total_cells, *refs), [shape((4, 16, WI...  4.39 us
    pallas_call x1, Pallas kernels, on_device(): call(forward_kernel, [shape((2, 6, W, CH), bf16), shape((SMALL + 48, CH),...  4.05 us
    ppermute x1, starting transfers between devices, on_device(): lax.ppermute(late, time_axes, [(i, i + 1) for i in range(shards - 1)])  3.4 us
    ppermute x1, waiting for transfers between devices, on_device(): down = lax.ppermute(top, row_axes, [(b, a) for a, b in lower])  3.29 us
    unnamed x18, local copies, waits for them, and re-layouts  2.78 us
  transfers between devices with their start and end apart: 5, of which 3 were waited for; matrix products, arithmetic and copies ran while one was open for 0% of the time, Pallas kernels for 6%

profile of v2, /device:TPU:2, one launch (start us, length us, event | category | flops | bytes accessed | tf_op | source)
XLA Modules:
  0.0 74.1 jit_solution(16464766079055070080)
XLA Ops:
  0.6 0.0 copy-start.1
  0.6 1.0 %copy-done.1 = bf16[4,4,128,128]{3,2,1,0:T(8,128)(2,1)S(1)} copy-done((bf16[4,4,128,128]{3,2,1,0:T(8,128)(2,1)S(1)}, bf16[4,4,128,128]{3,2,1,0:T(8,128)(2,1)}, u32[]{:S(2)}) %copy-start.1) | copy-done | bytes 524312
  1.7 0.0 copy-start.4
  1.7 0.0 copy-start
  1.7 0.0 copy-start.5
  1.7 0.0 copy-start.6
  1.7 0.0 copy-start.7
  1.7 0.0 copy-start.8
  1.7 0.2 shard_map.102
  1.9 1.9 %collective-permute-start = (bf16[4,128,128]{2,1,0:T(8,128)(2,1)S(1)}, bf16[4,128,128]{2,1,0:T(8,128)(2,1)S(1)}, u32[]{:S(2)}, u32[]{:S(2)}) collective-permute-start(bf16[4,128,128]{2,1,0:T(8,128)(2,1)S(1)} %get-tuple-element.18), channel_id=1, source_target_pairs={{0,1},{1,2},{2,3},{3,4},{4,5},{5,6},{6,7},{8,9},{9,10},{10,11},{11... | collective-permute-start | bytes 393224 | tf_op jit(solution)/shard_map/ppermute | solution.py:319
  3.8 1.3 %collective-permute-start.1 = (bf16[4,128,128]{2,1,0:T(8,128)(2,1)S(1)}, bf16[4,128,128]{2,1,0:T(8,128)(2,1)S(1)}, u32[]{:S(2)}, u32[]{:S(2)}) collective-permute-start(bf16[4,128,128]{2,1,0:T(8,128)(2,1)S(1)} %get-tuple-element.19), channel_id=1, source_target_pairs={{1,0},{2,1},{3,2},{4,3},{5,4},{6,5},{7,6},{9,8},{10,9},{11,10},{12... | collective-permute-start | bytes 393224 | tf_op jit(solution)/shard_map/ppermute | solution.py:320
  5.1 0.0 collective-permute-done.up_ref
  5.1 3.3 %collective-permute-done.1.down_ref = bf16[4,128,128]{2,1,0:T(8,128)(2,1)S(1)} collective-permute-done((bf16[4,128,128]{2,1,0:T(8,128)(2,1)S(1)}, bf16[4,128,128]{2,1,0:T(8,128)(2,1)S(1)}, u32[]{:S(2)}, u32[]{:S(2)}) %collective-permute-start.1) | collective-permute-done | bytes 131104 | tf_op jit(solution)/shard_map/ppermute | solution.py:320
  8.4 0.1 shard_map.103
  8.4 3.4 %collective-permute-start.2 = (bf16[2,6,128,128]{3,2,1,0:T(8,128)(2,1)S(1)}, bf16[2,6,128,128]{3,2,1,0:T(8,128)(2,1)S(1)}, u32[]{:S(2)}, u32[]{:S(2)}) collective-permute-start(bf16[2,6,128,128]{3,2,1,0:T(8,128)(2,1)S(1)} %get-tuple-element.20), channel_id=1, source_target_pairs={{0,8},{8,16},{16,24},{24,32},{32,40},{40,48},{48,56},{56,64},{64,7... | collective-permute-start | bytes 1179656 | tf_op jit(solution)/shard_map/ppermute | solution.py:327
  11.8 0.0 copy-done.4
  11.8 0.7 shard_map.105
  12.5 11.3 %all-to-all-start = ((f32[32,1,128]{2,1,0:T(1,128)}), f32[32,1,128]{2,1,0:T(1,128)S(1)}, u32[]{:S(2)}, u32[]{:S(2)}) async-start(f32[32,1,128]{2,1,0:T(1,128)} %bitcast.7), calls=%async_computation | async-start | bytes 32768 | tf_op jit(solution)/shard_map/all_to_all | solution.py:322
  23.8 0.0 collective-permute-done.2.earlier_ref
  23.8 0.0 copy-start.2
  23.9 0.7 copy-done.2
  24.6 0.0 copy-done
  24.6 0.0 copy-done.5
  24.6 0.0 copy-done.6
  24.6 0.0 copy-done.7
  24.6 0.0 copy-done.8
  24.6 0.0 copy-start.3
  24.6 1.0 %copy-done.3 = bf16[2,6,128,128]{3,2,1,0:T(8,128)(2,1)S(1)} copy-done((bf16[2,6,128,128]{3,2,1,0:T(8,128)(2,1)S(1)}, bf16[2,6,128,128]{3,2,1,0:T(8,128)(2,1)}, u32[]{:S(2)}) %copy-start.3) | copy-done | bytes 393240
  25.6 4.0 %shard_map.104 = (bf16[2,6,128,128]{3,2,1,0:T(8,128)(2,1)S(1)}, f32[2608,128]{1,0:T(8,128)S(1)}, f32[4,24,32]{2,1,0:T(8,128)}) custom-call(s32[6]{0:T(128)S(1)} %copy-done.7, s32[4,24,32]{2,1,0:T(8,128)S(1)} %bitcast.16, bf16[2,6,128,128]{3,2,1,0:T(8,128)(2,1)S(1)} %copy-done.3, bf16[4,6,128,128]{3,2,1,0:T(8,128)(2,1)S(1)} %get-tuple-element.21.x_ref.refs_1_, ...), custom_call_target="tpu_custom_call" | custom-call | tf_op jit(solution)/shard_map/pallas_call | solution.py:328
  29.7 2.7 %all-to-all-done = f32[32,1,128]{2,1,0:T(1,128)S(1)} async-done(((f32[32,1,128]{2,1,0:T(1,128)}), f32[32,1,128]{2,1,0:T(1,128)S(1)}, u32[]{:S(2)}, u32[]{:S(2)}) %all-to-all-start) | async-done | bytes 16416 | tf_op jit(solution)/shard_map/all_to_all | solution.py:322
  32.4 4.4 %shard_map.106 = (f32[4,16,3584]{2,1,0:T(8,128)S(1)}, f32[4,16,3584]{2,1,0:T(8,128)S(1)}) custom-call(bf16[2,6,128,128]{3,2,1,0:T(8,128)(2,1)S(1)} %get-tuple-element.23.refs_0_, bf16[4,6,128,128]{3,2,1,0:T(8,128)(2,1)S(1)} %get-tuple-element.21.x_ref.refs_1_, f32[2608,128]{1,0:T(8,128)S(1)} %get-tuple-element.24.refs_2_, f32[32,128]{1,0:T(8,128)S(1)} %bitcast.14), custom_call_target="tpu_custom_call" | custom-call | tf_op jit(solution)/shard_map/pallas_call | solution.py:351
  36.7 2.0 %collective-permute-start.3 = (f32[4,16,3584]{2,1,0:T(8,128)S(1)}, f32[4,16,3584]{2,1,0:T(8,128)S(1)}, u32[]{:S(2)}, u32[]{:S(2)}) collective-permute-start(f32[4,16,3584]{2,1,0:T(8,128)S(1)} %get-tuple-element.26), channel_id=1, source_target_pairs={{0,1},{1,0},{2,3},{3,2},{4,5},{5,4},{6,7},{7,6},{8,9},{9,8},{10,11... | collective-permute-start | bytes 2752520 | tf_op jit(solution)/shard_map/ppermute | solution.py:358
  38.7 2.1 %collective-permute-done.3.got_ref = f32[4,16,3584]{2,1,0:T(8,128)S(1)} collective-permute-done((f32[4,16,3584]{2,1,0:T(8,128)S(1)}, f32[4,16,3584]{2,1,0:T(8,128)S(1)}, u32[]{:S(2)}, u32[]{:S(2)}) %collective-permute-start.3) | collective-permute-done | bytes 917536 | tf_op jit(solution)/shard_map/ppermute | solution.py:358
  40.8 0.3 shard_map.107
  41.2 17.9 %all_to_all.15.parts_ref = bf16[16,144,128]{2,1,0:T(8,128)(2,1)S(1)} all-to-all(bf16[16,144,128]{2,1,0:T(8,128)(2,1)S(1)} %shard_map.107), channel_id=1, replica_groups=mesh['z'=8,'x'=4,'y'=4,'c'=2] {'x','y'}, dimensions={0} | all-to-all | bytes 1179648 | tf_op jit(solution)/shard_map/all_to_all | solution.py:360
  59.0 0.1 shard_map.108
  59.1 14.4 %all_to_all.16.parts_ref = f32[8,24,128]{2,1,0:T(8,128)S(1)} all-to-all(f32[8,24,128]{2,1,0:T(8,128)S(1)} %shard_map.108), channel_id=1, replica_groups=mesh['z'=8,'x'=4,'y'=4,'c'=2] {'z'}, dimensions={0} | all-to-all | bytes 196608 | tf_op jit(solution)/shard_map/all_to_all | solution.py:362
  73.5 0.6 shard_map.109
Async XLA Ops:
  0.6 1.0 %copy-start.1 = (bf16[4,4,128,128]{3,2,1,0:T(8,128)(2,1)S(1)}, bf16[4,4,128,128]{3,2,1,0:T(8,128)(2,1)}, u32[]{:S(2)}) copy-start(bf16[4,4,128,128]{3,2,1,0:T(8,128)(2,1)} %frames_any.1) | copy-start | bytes 1572868
  1.7 10.2 %copy-start.4 = (f32[32,4,24]{0,2,1:T(8,128)S(1)}, f32[32,4,24]{0,2,1:T(8,128)}, u32[]{:S(2)}) copy-start(f32[32,4,24]{0,2,1:T(8,128)} %param.13) | copy-start | bytes 36868
  1.7 22.9 %copy-start = (bf16[3456,128]{1,0:T(8,128)(2,1)S(1)}, bf16[3456,128]{1,0:T(8,128)(2,1)}, u32[]{:S(2)}) copy-start(bf16[3456,128]{1,0:T(8,128)(2,1)} %param.8) | copy-start | bytes 2654212
  1.7 22.9 %copy-start.5 = (s32[32,4,24]{0,2,1:T(8,128)S(1)}, s32[32,4,24]{0,2,1:T(8,128)}, u32[]{:S(2)}) copy-start(s32[32,4,24]{0,2,1:T(8,128)} %param.12) | copy-start | bytes 36868
  1.7 22.9 %copy-start.6 = (f32[128,6]{0,1:T(8,128)S(1)}, f32[128,6]{0,1:T(8,128)}, u32[]{:S(2)}) copy-start(f32[128,6]{0,1:T(8,128)} %param.10) | copy-start | bytes 9220
  1.7 22.9 %copy-start.7 = (s32[6]{0:T(128)S(1)}, s32[6]{0:T(128)}, u32[]{:S(2)}) copy-start(s32[6]{0:T(128)} %levels_any.1) | copy-start | bytes 76
  1.7 22.9 %copy-start.8 = (f32[128]{0:T(128)S(1)}, f32[128]{0:T(128)}, u32[]{:S(2)}) copy-start(f32[128]{0:T(128)} %param.9) | copy-start | bytes 1540
  1.9 3.2 %collective-permute-start = (bf16[4,128,128]{2,1,0:T(8,128)(2,1)S(1)}, bf16[4,128,128]{2,1,0:T(8,128)(2,1)S(1)}, u32[]{:S(2)}, u32[]{:S(2)}) collective-permute-start(bf16[4,128,128]{2,1,0:T(8,128)(2,1)S(1)} %get-tuple-element.18), channel_id=1, source_target_pairs={{0,1},{1,2},{2,3},{3,4},{4,5},{5,6},{6,7},{8,9},{9,10},{10,11},{11... | collective-permute-start | bytes 393224 | tf_op jit(solution)/shard_map/ppermute | solution.py:319
  3.8 4.6 %collective-permute-start.1 = (bf16[4,128,128]{2,1,0:T(8,128)(2,1)S(1)}, bf16[4,128,128]{2,1,0:T(8,128)(2,1)S(1)}, u32[]{:S(2)}, u32[]{:S(2)}) collective-permute-start(bf16[4,128,128]{2,1,0:T(8,128)(2,1)S(1)} %get-tuple-element.19), channel_id=1, source_target_pairs={{1,0},{2,1},{3,2},{4,3},{5,4},{6,5},{7,6},{9,8},{10,9},{11,10},{12... | collective-permute-start | bytes 393224 | tf_op jit(solution)/shard_map/ppermute | solution.py:320
  8.4 15.4 %collective-permute-start.2 = (bf16[2,6,128,128]{3,2,1,0:T(8,128)(2,1)S(1)}, bf16[2,6,128,128]{3,2,1,0:T(8,128)(2,1)S(1)}, u32[]{:S(2)}, u32[]{:S(2)}) collective-permute-start(bf16[2,6,128,128]{3,2,1,0:T(8,128)(2,1)S(1)} %get-tuple-element.20), channel_id=1, source_target_pairs={{0,8},{8,16},{16,24},{24,32},{32,40},{40,48},{48,56},{56,64},{64,7... | collective-permute-start | bytes 1179656 | tf_op jit(solution)/shard_map/ppermute | solution.py:327
  12.5 19.8 %all-to-all-start = ((f32[32,1,128]{2,1,0:T(1,128)}), f32[32,1,128]{2,1,0:T(1,128)S(1)}, u32[]{:S(2)}, u32[]{:S(2)}) async-start(f32[32,1,128]{2,1,0:T(1,128)} %bitcast.7), calls=%async_computation | async-start | bytes 32768 | tf_op jit(solution)/shard_map/all_to_all | solution.py:322
  23.8 0.7 %copy-start.2 = (bf16[2,6,128,128]{3,2,1,0:T(8,128)(2,1)}, bf16[2,6,128,128]{3,2,1,0:T(8,128)(2,1)S(1)}, u32[]{:S(2)}) copy-start(bf16[2,6,128,128]{3,2,1,0:T(8,128)(2,1)S(1)} %collective-permute-done.2.earlier_ref) | copy-start | bytes 1179652
  24.6 1.0 %copy-start.3 = (bf16[2,6,128,128]{3,2,1,0:T(8,128)(2,1)S(1)}, bf16[2,6,128,128]{3,2,1,0:T(8,128)(2,1)}, u32[]{:S(2)}) copy-start(bf16[2,6,128,128]{3,2,1,0:T(8,128)(2,1)} %copy-done.2) | copy-start | bytes 1179652
  36.7 4.1 %collective-permute-start.3 = (f32[4,16,3584]{2,1,0:T(8,128)S(1)}, f32[4,16,3584]{2,1,0:T(8,128)S(1)}, u32[]{:S(2)}, u32[]{:S(2)}) collective-permute-start(f32[4,16,3584]{2,1,0:T(8,128)S(1)} %get-tuple-element.26), channel_id=1, source_target_pairs={{0,1},{1,0},{2,3},{3,2},{4,5},{5,4},{6,7},{7,6},{8,9},{9,8},{10,11... | collective-permute-start | bytes 2752520 | tf_op jit(solution)/shard_map/ppermute | solution.py:358

commit v3 on v2

--- a/solution.py
+++ b/solution.py
@@ -48,7 +48,7 @@
 def half_ranges(levels_ref, channel):
     half = jnp.ones(channel.shape, f32)
     for j in range(L):
-        half = jnp.where(channel == j, (levels_ref[j].astype(f32) - 1.0) * 0.5, half)
+        half = jnp.where(channel == j, (levels_ref[:, j : j + 1].astype(f32) - 1.0) * 0.5, half)
     return half
 
 
@@ -59,26 +59,42 @@
     codes_ref[...] = padded.T[:frames]
 
 
-def edge_kernel(frames_any, x_ref, top_ref, bottom_ref, sems):
+def edge_kernel(frames_any, x_ref, inner_ref, outer_ref, sems):
+    core = lax.axis_index("c")
     copy_all(
         [
             (frames_any, x_ref.at[:, 1:5]),
-            (frames_any.at[:, 0], top_ref),
-            (frames_any.at[:, 3], bottom_ref),
+            (frames_any.at[:, 3 - 3 * core], inner_ref),
+            (frames_any.at[:, 3 * core], outer_ref),
         ],
         sems,
     )
 
 
-def late_kernel(own_ref, up_ref, down_ref, x_ref, late_ref):
+def late_kernel(own_ref, inner_ref, outer_ref, code_any, x_ref, late_ref):
+    core = lax.axis_index("c")
+    inner_row, outer_row = 5 - 5 * core, 5 * core
     for t in range(4):
-        x_ref[t, 0] = up_ref[t]
-        x_ref[t, 5] = down_ref[t]
+        x_ref[t, inner_row] = inner_ref[t]
+        x_ref[t, outer_row] = outer_ref[t]
     for t in range(2):
-        late_ref[t, 0] = up_ref[t + 2]
-        late_ref[t, 5] = down_ref[t + 2]
+        late_ref[t, inner_row] = inner_ref[t + 2]
+        late_ref[t, outer_row] = outer_ref[t + 2]
         for h in range(1, 5):
             late_ref[t, h] = own_ref[t + 2, h]
+
+
+def early_kernel(earlier_ref, x_ref, early_ref):
+    first = (lax.axis_index("z") == 0) & (lax.axis_index("x") == 0)
+
+    @pl.when(first)
+    def _():
+        for t in range(2):
+            early_ref[t] = x_ref[0]
+
+    @pl.when(jnp.logical_not(first))
+    def _():
+        early_ref[...] = earlier_ref[...]
 
 
 def block_of(early_ref, x_ref):
@@ -100,55 +116,27 @@
 
 
 def forward_kernel(
-    levels_any,
-    centres_any,
-    earlier_ref,
+    levels_ref,
+    centres_ref,
+    early_ref,
     x_ref,
-    weight_any,
-    bias_any,
-    projection_any,
-    early_ref,
+    weight_ref,
+    bias_ref,
+    projection_ref,
     state_ref,
     quantized_ref,
-    wide_ref,
-    levels_ref,
-    centres_ref,
-    bias_ref,
-    projection_ref,
-    sems,
 ):
-    first = (lax.axis_index("z") == 0) & (lax.axis_index("x") == 0)
-    copy_all(
-        [
-            (weight_any.at[:, 0], wide_ref.at[:, :, 0:CH]),
-            (weight_any.at[:, 1], wide_ref.at[:, :, CH : 2 * CH]),
-            (weight_any.at[:, 2], wide_ref.at[:, :, 2 * CH : 3 * CH]),
-            (levels_any, levels_ref),
-            (centres_any, centres_ref),
-            (bias_any, bias_ref),
-            (projection_any, projection_ref.at[0:L]),
-        ],
-        sems,
-    )
-    projection_ref[L:8] = jnp.zeros((8 - L, CH), f32)
     rows, columns, groups = centres_ref.shape
     channel = lax.broadcasted_iota(jnp.int32, (columns, groups), 0) % L
     half = half_ranges(levels_ref, channel)
     for h in range(rows):
         quantized_ref[h] = (centres_ref[h].astype(f32) - half) / half
 
-    @pl.when(first)
-    def _():
-        for t in range(2):
-            early_ref[t] = x_ref[0]
-
-    @pl.when(jnp.logical_not(first))
-    def _():
-        early_ref[...] = earlier_ref[...]
-
     block = block_of(early_ref, x_ref)
 
-    wide = wide_ref[...].reshape(9 * CH, 3 * CH)
+    wide = jnp.concatenate(
+        [jnp.concatenate([weight_ref[tap, c] for c in range(3)], 1) for tap in range(9)], 0
+    )
     bias = bias_ref[...]
     pooled = [jnp.zeros((W, CH), f32) for _ in range(4)]
     for t in range(4):
@@ -161,13 +149,13 @@
                 + z[:, CH : 2 * CH]
                 + shifted_rows(z[:, 2 * CH :], -1)
             )
-            sigmoid = 1.0 / (1.0 + jnp.exp(-preact))
+            sigmoid = 0.5 * jnp.tanh(0.5 * preact) + 0.5
             place = (t * 4 + h) * W
             state_ref[place : place + W] = sigmoid * (1.0 + preact * (1.0 - sigmoid))
             pooled[h] = pooled[h] + (preact * sigmoid).astype(bf16).astype(f32)
     pooled = jnp.concatenate(pooled, 0) * 0.25
     state_ref[STATE : STATE + 4 * W] = pooled
-    projection = projection_ref[...]
+    projection = jnp.concatenate([projection_ref[...], jnp.zeros((8 - L, CH), f32)], 0)
     latent = lax.dot_general(
         projection, pooled, (((1,), (1,)), ((), ())), precision=highest, preferred_element_type=f32
     )
@@ -196,10 +184,9 @@
     x_ref,
     state_ref,
     code_ref,
-    mine_ref,
     theirs_ref,
     low_ref,
-    grad_ref,
+    small_ref,
 ):
     core = lax.axis_index("c")
     pooled = state_ref[STATE : STATE + 4 * W]
@@ -245,25 +232,34 @@
     bias_row = bias_part.sum(0, keepdims=True)
     row = lax.broadcasted_iota(jnp.int32, (8, CH), 0)
     small = jnp.where(row == L, bias_row, projection_part)
+    small_ref[...] = small
+    kernel_gradient(1 - core, early_ref, x_ref, low_ref, theirs_ref)
+    for y in range(4):
+        theirs_ref[y, 0:8, LANES:] = small
+        theirs_ref[y, 8:16, LANES:] = jnp.zeros((8, CH), f32)
+
+
+def kernel_gradient(core, early_ref, x_ref, low_ref, out_ref):
+    starts = [pl.multiple_of(c * CH + 32 * y + 16 * core, 16) for c in range(3) for y in range(4)]
+    left = jnp.concatenate([low_ref[pl.ds(start, 16), :] for start in starts], 0)
     taps = [(a, b) for a in range(3) for b in range(3)]
     for start in range(0, 9, 2):
         group = taps[start : start + 2]
         right = jnp.concatenate([window(early_ref, x_ref, a, b) for a, b in group], 1)
-        grad_ref[:, start * CH : (start + len(group)) * CH] = jnp.dot(
-            low_ref[...], right, preferred_element_type=f32
-        )
+        result = jnp.dot(left, right, preferred_element_type=f32)
+        for place in range(len(group)):
+            for c in range(3):
+                to = slice((3 * (start + place) + c) * CH, (3 * (start + place) + c + 1) * CH)
+                for y in range(4):
+                    row = (c * 4 + y) * 16
+                    out_ref[y, :, to] = result[row : row + 16, place * CH : (place + 1) * CH]
+
+
+def own_kernel(early_ref, x_ref, low_ref, small_ref, mine_ref):
+    kernel_gradient(lax.axis_index("c"), early_ref, x_ref, low_ref, mine_ref)
     for y in range(4):
-        for c in range(3):
-            own = pl.multiple_of(c * CH + 32 * y + 16 * core, 16)
-            other = pl.multiple_of(c * CH + 32 * y + 16 * (1 - core), 16)
-            for tap in range(9):
-                to = slice((3 * tap + c) * CH, (3 * tap + c + 1) * CH)
-                mine_ref[y, :, to] = grad_ref[pl.ds(own, 16), tap * CH : (tap + 1) * CH]
-                theirs_ref[y, :, to] = grad_ref[pl.ds(other, 16), tap * CH : (tap + 1) * CH]
-        mine_ref[y, 0:8, LANES:] = small
+        mine_ref[y, 0:8, LANES:] = small_ref[...]
         mine_ref[y, 8:16, LANES:] = jnp.zeros((8, CH), f32)
-        theirs_ref[y, 0:8, LANES:] = small
-        theirs_ref[y, 8:16, LANES:] = jnp.zeros((8, CH), f32)
 
 
 def pair_kernel(mine_ref, got_ref, out_ref):
@@ -312,35 +308,29 @@
 
     code_grad = jnp.transpose(code_grad, (1, 2, 0))
     centres = jnp.transpose(centres, (1, 2, 0))
-    lower = [(i, i + 1) for i in range(strips - 1)]
+    crossing = [(i, i + 1) for i in range(1, strips - 1, 2)]
+    crossing = crossing + [(b, a) for a, b in crossing]
     edge = shape((4, W, CH), bf16)
     own = shape((4, 6, W, CH), bf16)
-    x, top, bottom = call(edge_kernel, [own, edge, edge], [ANY], [dma((3,))])(frames)
-    up = lax.ppermute(bottom, row_axes, lower)
-    down = lax.ppermute(top, row_axes, [(b, a) for a, b in lower])
+    x, inner, outer = call(edge_kernel, [own, edge, edge], [ANY], [dma((3,))])(frames)
+    outer = lax.ppermute(outer, row_axes, crossing)
+    inner = lax.ppermute(inner, "c", [(0, 1), (1, 0)])
     (codes,) = call(code_kernel, [shape((shards, CH), f32)], [VMEM])(code_grad)
+    x, late = call(
+        late_kernel, [own, shape((2, 6, W, CH), bf16)], [VMEM] * 3 + [ANY], aliases={0: 0}
+    )(x, inner, outer, codes)
     codes = lax.all_to_all(codes.reshape(shards, 1, CH), time_axes, 0, 0, tiled=True)
     codes = codes.reshape(shards, CH)
-    x, late = call(
-        late_kernel, [own, shape((2, 6, W, CH), bf16)], [VMEM] * 3, aliases={0: 0}
-    )(x, up, down)
     earlier = lax.ppermute(late, time_axes, [(i, i + 1) for i in range(shards - 1)])
-    early, state, quantized = call(
+    (early,) = call(early_kernel, [shape((2, 6, W, CH), bf16)], [VMEM] * 2)(earlier, x)
+    state, quantized = call(
         forward_kernel,
-        [shape((2, 6, W, CH), bf16), shape((SMALL + 48, CH), f32), shape(centres.shape, f32)],
-        [ANY] * 2 + [VMEM] * 2 + [ANY] * 3,
-        [
-            pltpu.VMEM((9, CH, 3 * CH), bf16),
-            pltpu.SMEM((L,), jnp.int32),
-            pltpu.VMEM(centres.shape, jnp.int32),
-            pltpu.VMEM((1, CH), f32),
-            pltpu.VMEM((8, CH), f32),
-            dma((7,)),
-        ],
+        [shape((SMALL + 48, CH), f32), shape(centres.shape, f32)],
+        [VMEM] * 7,
     )(
-        levels,
+        levels.reshape(1, L),
         centres,
-        earlier,
+        early,
         x,
         conv_weight.reshape(9, 3, CH, CH),
         conv_bias.reshape(1, CH),
@@ -348,14 +338,14 @@
     )
 
     total_cells = 4 * shards * 4 * strips * W
-    mine, theirs = call(
+    theirs, low, small = call(
         lambda *refs: backward_kernel(total_cells, *refs),
-        [shape((4, 16, WIDE), f32)] * 2,
+        [shape((4, 16, WIDE), f32), shape((3 * CH, 16 * W), bf16), shape((8, CH), f32)],
         [VMEM] * 4,
-        [pltpu.VMEM((3 * CH, 16 * W), bf16), pltpu.VMEM((3 * CH, 9 * CH), f32)],
     )(early, x, state, codes)
 
     got = lax.ppermute(theirs, "c", [(0, 1), (1, 0)])
+    (mine,) = call(own_kernel, [shape((4, 16, WIDE), f32)], [VMEM] * 4)(early, x, low, small)
     (chunks,) = call(pair_kernel, [shape((16, 144, CH), bf16)], [VMEM] * 2)(mine, got)
     chunks = lax.all_to_all(chunks, ("x", "y"), 0, 0, tiled=True)
     (chunks,) = call(plane_kernel, [shape((8, 24, CH), f32)], [VMEM])(chunks)

time: 74.5 us -> 69.2 us (0.929)
  waiting for transfers between devices: 8.08 us -> 5.49 us
  starting transfers between devices: 19.9 us -> 18.5 us
  local copies, waits for them, and re-layouts: 2.78 us -> 1.85 us
    ppermute x2, waiting for transfers between devices: 3.29 us -> 0.01 us  [the longest x1 0.01 us: on_device(): inner = lax.ppermute(inner, 'c', [(0, 1), (1, 0)])]
    ppermute x2, starting transfers between devices: 3.17 us -> 0.76 us  [the longest x1 0.67 us: on_device(): outer = lax.ppermute(outer, row_axes, crossing)]
    all_to_all x1, waiting for transfers between devices: 2.69 us -> 4.59 us  [on_device(): lax.all_to_all(codes.reshape(shards, 1, CH), time_axes, 0, 0, tiled=True)]
    all_to_all x1, blocking collectives: 14.4 us -> 13 us  [on_device(): parts = lax.all_to_all(chunks, 'z', 0, 0, tiled=True)]
    all_to_all x1, blocking collectives: 17.9 us -> 19.1 us  [on_device(): chunks = lax.all_to_all(chunks, ('x', 'y'), 0, 0, tiled=True)]
    ppermute x1, waiting for transfers between devices: 2.1 us -> 0.89 us  [on_device(): got = lax.ppermute(theirs, 'c', [(0, 1), (1, 0)])]
    pallas_call x1, Pallas kernels: 4.39 us -> 3.21 us  [on_device(): call(lambda *refs: backward_kernel(total_cells, *refs), [shape((4, 16, WI...]
    pallas_call x2 -> x4, Pallas kernels: 4.11 us -> 5.14 us  [the longest x1 3.82 us: on_device(): call(forward_kernel, [shape((SMALL + 48, CH), f32), shape(centres.shape,...]
  transfers between devices with their start and end apart: 5 -> 5, of which waited for: 3 -> 2; matrix products, arithmetic and copies ran while one was open for 0% -> 0% of each run, Pallas kernels for 6% -> 8%
where the time goes in v3:
time: 69.2 us; the launch traced here: 68.9 us
  blocking collectives  32.1 us (46%)
  starting transfers between devices  18.5 us (27%)
  Pallas kernels  10.2 us (15%)
  waiting for transfers between devices  5.49 us (8%)
  local copies, waits for them, and re-layouts  1.85 us (3%)
  between operations  0.78 us (1%)
    all_to_all x1, blocking collectives, on_device(): chunks = lax.all_to_all(chunks, ('x', 'y'), 0, 0, tiled=True)  19.1 us
    all_to_all x1, blocking collectives, on_device(): parts = lax.all_to_all(chunks, 'z', 0, 0, tiled=True)  13 us
    all_to_all x1, starting transfers between devices, on_device(): lax.all_to_all(codes.reshape(shards, 1, CH), time_axes, 0, 0, tiled=True)  11.3 us
    all_to_all x1, waiting for transfers between devices, on_device(): lax.all_to_all(codes.reshape(shards, 1, CH), time_axes, 0, 0, tiled=True)  4.59 us
    pallas_call x1, Pallas kernels, on_device(): call(forward_kernel, [shape((SMALL + 48, CH), f32), shape(centres.shape,...  3.82 us
    ppermute x1, starting transfers between devices, on_device(): lax.ppermute(late, time_axes, [(i, i + 1) for i in range(shards - 1)])  3.4 us
    pallas_call x1, Pallas kernels, on_device(): call(lambda *refs: backward_kernel(total_cells, *refs), [shape((4, 16, WI...  3.21 us
    ppermute x1, starting transfers between devices, on_device(): got = lax.ppermute(theirs, 'c', [(0, 1), (1, 0)])  2.98 us
  transfers between devices with their start and end apart: 5, of which 2 were waited for; matrix products, arithmetic and copies ran while one was open for 0% of the time, Pallas kernels for 8%

profile of v3, /device:TPU:2, one launch (start us, length us, event | category | flops | bytes accessed | tf_op | source)
XLA Modules:
  0.0 68.9 jit_solution(647381811399990837)
XLA Ops:
  0.6 0.0 copy-start.1
  0.6 1.0 %copy-done.1 = bf16[4,4,128,128]{3,2,1,0:T(8,128)(2,1)S(1)} copy-done((bf16[4,4,128,128]{3,2,1,0:T(8,128)(2,1)S(1)}, bf16[4,4,128,128]{3,2,1,0:T(8,128)(2,1)}, u32[]{:S(2)}) %copy-start.1) | copy-done | bytes 524312
  1.7 0.0 copy-start
  1.7 0.1 shard_map.102
  1.8 0.1 collective-permute-start
  1.9 0.7 collective-permute-start.1
  2.6 0.0 copy-start.2
  2.6 0.8 %copy-done.2 = f32[32,4,24]{0,2,1:T(8,128)S(1)} copy-done((f32[32,4,24]{0,2,1:T(8,128)S(1)}, f32[32,4,24]{0,2,1:T(8,128)}, u32[]{:S(2)}) %copy-start.2) | copy-done | bytes 12312
  3.4 0.0 copy-start.3
  3.4 0.0 copy-start.4
  3.4 0.0 copy-start.5
  3.4 0.0 copy-start.6
  3.4 0.7 shard_map.103.code_any
  4.1 0.0 collective-permute-done.inner_ref
  4.1 0.0 collective-permute-done.1.outer_ref
  4.1 0.1 shard_map.104
  4.2 3.4 %collective-permute-start.2 = (bf16[2,6,128,128]{3,2,1,0:T(8,128)(2,1)S(1)}, bf16[2,6,128,128]{3,2,1,0:T(8,128)(2,1)S(1)}, u32[]{:S(2)}, u32[]{:S(2)}) collective-permute-start(bf16[2,6,128,128]{3,2,1,0:T(8,128)(2,1)S(1)} %get-tuple-element.20), channel_id=1, source_target_pairs={{0,8},{8,16},{16,24},{24,32},{32,40},{40,48},{48,56},{56,64},{64,7... | collective-permute-start | bytes 1179656 | tf_op jit(solution)/shard_map/ppermute | solution.py:324
  7.6 11.3 %all-to-all-start = ((f32[32,1,128]{2,1,0:T(1,128)}), f32[32,1,128]{2,1,0:T(1,128)S(1)}, u32[]{:S(2)}, u32[]{:S(2)}) async-start(f32[32,1,128]{2,1,0:T(1,128)} %bitcast.8), calls=%async_computation | async-start | bytes 32768 | tf_op jit(solution)/shard_map/all_to_all | solution.py:322
  18.9 0.0 collective-permute-done.2.earlier_ref
  19.0 0.0 copy-done
  19.0 0.0 copy-done.3
  19.0 0.0 copy-done.4
  19.0 0.0 copy-done.5
  19.0 0.0 copy-done.6
  19.0 3.8 %shard_map.106 = (f32[2608,128]{1,0:T(8,128)S(1)}, f32[4,24,32]{2,1,0:T(8,128)}) custom-call(s32[1,6]{1,0:T(1,128)S(1)} %bitcast.19, s32[4,24,32]{2,1,0:T(8,128)S(1)} %bitcast.17, bf16[2,6,128,128]{3,2,1,0:T(8,128)(2,1)S(1)} %shard_map.105.early_ref.refs_0_, bf16[4,6,128,128]{3,2,1,0:T(8,128)(2,1)S(1)} %get-tuple-element.21.x_ref.refs_1_, ...), custom_call_target="tpu_custom_call" | custom-call | tf_op jit(solution)/shard_map/pallas_call | solution.py:326
  22.9 4.6 %all-to-all-done = f32[32,1,128]{2,1,0:T(1,128)S(1)} async-done(((f32[32,1,128]{2,1,0:T(1,128)}), f32[32,1,128]{2,1,0:T(1,128)S(1)}, u32[]{:S(2)}, u32[]{:S(2)}) %all-to-all-start) | async-done | bytes 16416 | tf_op jit(solution)/shard_map/all_to_all | solution.py:322
  27.5 3.2 %shard_map.107 = (f32[4,16,3584]{2,1,0:T(8,128)S(1)}, bf16[384,2048]{1,0:T(8,128)(2,1)S(1)}, f32[8,128]{1,0:T(8,128)S(1)}) custom-call(bf16[2,6,128,128]{3,2,1,0:T(8,128)(2,1)S(1)} %shard_map.105.early_ref.refs_0_, bf16[4,6,128,128]{3,2,1,0:T(8,128)(2,1)S(1)} %get-tuple-element.21.x_ref.refs_1_, f32[2608,128]{1,0:T(8,128)S(1)} %get-tuple-element.23.refs_2_, ...), custom_call_target="tpu_custom_call" | custom-call | tf_op jit(solution)/shard_map/pallas_call | solution.py:341
  30.7 3.0 %collective-permute-start.3 = (f32[4,16,3584]{2,1,0:T(8,128)S(1)}, f32[4,16,3584]{2,1,0:T(8,128)S(1)}, u32[]{:S(2)}, u32[]{:S(2)}) collective-permute-start(f32[4,16,3584]{2,1,0:T(8,128)S(1)} %get-tuple-element.26), channel_id=1, source_target_pairs={{0,1},{1,0},{2,3},{3,2},{4,5},{5,4},{6,7},{7,6},{8,9},{9,8},{10,11... | collective-permute-start | bytes 2752520 | tf_op jit(solution)/shard_map/ppermute | solution.py:347
  33.6 1.2 %shard_map.108.mine_ref = f32[4,16,3584]{2,1,0:T(8,128)S(1)} custom-call(bf16[2,6,128,128]{3,2,1,0:T(8,128)(2,1)S(1)} %shard_map.105.early_ref.refs_0_, bf16[4,6,128,128]{3,2,1,0:T(8,128)(2,1)S(1)} %get-tuple-element.21.x_ref.refs_1_, bf16[384,2048]{1,0:T(8,128)(2,1)S(1)} %get-tuple-element.24.low_ref, f32[8,128]{1,0:T(8,128)S(1)} %get-tuple-element.25.small_ref), custom_call_target="tpu_custom_call" | custom-call | tf_op jit(solution)/shard_map/pallas_call | solution.py:348
  34.9 0.9 %collective-permute-done.3.got_ref = f32[4,16,3584]{2,1,0:T(8,128)S(1)} collective-permute-done((f32[4,16,3584]{2,1,0:T(8,128)S(1)}, f32[4,16,3584]{2,1,0:T(8,128)S(1)}, u32[]{:S(2)}, u32[]{:S(2)}) %collective-permute-start.3) | collective-permute-done | bytes 917536 | tf_op jit(solution)/shard_map/ppermute | solution.py:347
  35.7 0.3 shard_map.109
  36.1 19.1 %all_to_all.15.parts_ref = bf16[16,144,128]{2,1,0:T(8,128)(2,1)S(1)} all-to-all(bf16[16,144,128]{2,1,0:T(8,128)(2,1)S(1)} %shard_map.109), channel_id=1, replica_groups=mesh['z'=8,'x'=4,'y'=4,'c'=2] {'x','y'}, dimensions={0} | all-to-all | bytes 1179648 | tf_op jit(solution)/shard_map/all_to_all | solution.py:350
  55.2 0.1 shard_map.110
  55.3 13.0 %all_to_all.16.parts_ref = f32[8,24,128]{2,1,0:T(8,128)S(1)} all-to-all(f32[8,24,128]{2,1,0:T(8,128)S(1)} %shard_map.110), channel_id=1, replica_groups=mesh['z'=8,'x'=4,'y'=4,'c'=2] {'z'}, dimensions={0} | all-to-all | bytes 196608 | tf_op jit(solution)/shard_map/all_to_all | solution.py:352
  68.3 0.6 shard_map.111
  (1 shorter events, 0.0 us)
Async XLA Ops:
  0.6 1.0 %copy-start.1 = (bf16[4,4,128,128]{3,2,1,0:T(8,128)(2,1)S(1)}, bf16[4,4,128,128]{3,2,1,0:T(8,128)(2,1)}, u32[]{:S(2)}) copy-start(bf16[4,4,128,128]{3,2,1,0:T(8,128)(2,1)} %frames_any.1) | copy-start | bytes 1572868
  1.7 17.3 %copy-start = (bf16[3456,128]{1,0:T(8,128)(2,1)S(1)}, bf16[3456,128]{1,0:T(8,128)(2,1)}, u32[]{:S(2)}) copy-start(bf16[3456,128]{1,0:T(8,128)(2,1)} %param.8) | copy-start | bytes 2654212
  1.8 2.3 %collective-permute-start = (bf16[4,128,128]{2,1,0:T(8,128)(2,1)S(1)}, bf16[4,128,128]{2,1,0:T(8,128)(2,1)S(1)}, u32[]{:S(2)}, u32[]{:S(2)}) collective-permute-start(bf16[4,128,128]{2,1,0:T(8,128)(2,1)S(1)} %get-tuple-element.18), channel_id=1, source_target_pairs={{0,1},{1,0},{2,3},{3,2},{4,5},{5,4},{6,7},{7,6},{8,9},{9,8},{10,11... | collective-permute-start | bytes 393224 | tf_op jit(solution)/shard_map/ppermute | solution.py:317
  1.9 2.2 %collective-permute-start.1 = (bf16[4,128,128]{2,1,0:T(8,128)(2,1)S(1)}, bf16[4,128,128]{2,1,0:T(8,128)(2,1)S(1)}, u32[]{:S(2)}, u32[]{:S(2)}) collective-permute-start(bf16[4,128,128]{2,1,0:T(8,128)(2,1)S(1)} %get-tuple-element.19), channel_id=1, source_target_pairs={{1,2},{3,4},{5,6},{2,1},{4,3},{6,5},{9,10},{11,12},{13,14},{10,9},... | collective-permute-start | bytes 393224 | tf_op jit(solution)/shard_map/ppermute | solution.py:316
  2.6 0.8 %copy-start.2 = (f32[32,4,24]{0,2,1:T(8,128)S(1)}, f32[32,4,24]{0,2,1:T(8,128)}, u32[]{:S(2)}) copy-start(f32[32,4,24]{0,2,1:T(8,128)} %param.13) | copy-start | bytes 36868
  3.4 15.6 %copy-start.3 = (s32[32,4,24]{0,2,1:T(8,128)S(1)}, s32[32,4,24]{0,2,1:T(8,128)}, u32[]{:S(2)}) copy-start(s32[32,4,24]{0,2,1:T(8,128)} %param.12) | copy-start | bytes 36868
  3.4 15.6 %copy-start.4 = (f32[128,6]{0,1:T(8,128)S(1)}, f32[128,6]{0,1:T(8,128)}, u32[]{:S(2)}) copy-start(f32[128,6]{0,1:T(8,128)} %param.10) | copy-start | bytes 9220
  3.4 15.6 %copy-start.5 = (s32[6]{0:T(128)S(1)}, s32[6]{0:T(128)}, u32[]{:S(2)}) copy-start(s32[6]{0:T(128)} %param.11) | copy-start | bytes 76
  3.4 15.6 %copy-start.6 = (f32[128]{0:T(128)S(1)}, f32[128]{0:T(128)}, u32[]{:S(2)}) copy-start(f32[128]{0:T(128)} %param.9) | copy-start | bytes 1540
  4.2 14.8 %collective-permute-start.2 = (bf16[2,6,128,128]{3,2,1,0:T(8,128)(2,1)S(1)}, bf16[2,6,128,128]{3,2,1,0:T(8,128)(2,1)S(1)}, u32[]{:S(2)}, u32[]{:S(2)}) collective-permute-start(bf16[2,6,128,128]{3,2,1,0:T(8,128)(2,1)S(1)} %get-tuple-element.20), channel_id=1, source_target_pairs={{0,8},{8,16},{16,24},{24,32},{32,40},{40,48},{48,56},{56,64},{64,7... | collective-permute-start | bytes 1179656 | tf_op jit(solution)/shard_map/ppermute | solution.py:324
  7.6 19.9 %all-to-all-start = ((f32[32,1,128]{2,1,0:T(1,128)}), f32[32,1,128]{2,1,0:T(1,128)S(1)}, u32[]{:S(2)}, u32[]{:S(2)}) async-start(f32[32,1,128]{2,1,0:T(1,128)} %bitcast.8), calls=%async_computation | async-start | bytes 32768 | tf_op jit(solution)/shard_map/all_to_all | solution.py:322
  30.7 5.1 %collective-permute-start.3 = (f32[4,16,3584]{2,1,0:T(8,128)S(1)}, f32[4,16,3584]{2,1,0:T(8,128)S(1)}, u32[]{:S(2)}, u32[]{:S(2)}) collective-permute-start(f32[4,16,3584]{2,1,0:T(8,128)S(1)} %get-tuple-element.26), channel_id=1, source_target_pairs={{0,1},{1,0},{2,3},{3,2},{4,5},{5,4},{6,7},{7,6},{8,9},{9,8},{10,11... | collective-permute-start | bytes 2752520 | tf_op jit(solution)/shard_map/ppermute | solution.py:347

commit v4 on v3

--- a/solution.py
+++ b/solution.py
@@ -59,32 +59,30 @@
     codes_ref[...] = padded.T[:frames]
 
 
-def edge_kernel(frames_any, x_ref, inner_ref, outer_ref, sems):
+def edge_kernel(frames_any, x_ref, inner_ref, outer_ref, late_ref, sems):
     core = lax.axis_index("c")
     copy_all(
         [
             (frames_any, x_ref.at[:, 1:5]),
             (frames_any.at[:, 3 - 3 * core], inner_ref),
             (frames_any.at[:, 3 * core], outer_ref),
+            (frames_any.at[2:4], late_ref),
         ],
         sems,
     )
 
 
-def late_kernel(own_ref, inner_ref, outer_ref, code_any, x_ref, late_ref):
+def rim_kernel(own_ref, inner_ref, outer_ref, code_any, x_ref, rim_ref):
     core = lax.axis_index("c")
-    inner_row, outer_row = 5 - 5 * core, 5 * core
     for t in range(4):
-        x_ref[t, inner_row] = inner_ref[t]
-        x_ref[t, outer_row] = outer_ref[t]
+        x_ref[t, 5 - 5 * core] = inner_ref[t]
+        x_ref[t, 5 * core] = outer_ref[t]
     for t in range(2):
-        late_ref[t, inner_row] = inner_ref[t + 2]
-        late_ref[t, outer_row] = outer_ref[t + 2]
-        for h in range(1, 5):
-            late_ref[t, h] = own_ref[t + 2, h]
-
-
-def early_kernel(earlier_ref, x_ref, early_ref):
+        rim_ref[t, 1 - core] = inner_ref[t + 2]
+        rim_ref[t, core] = outer_ref[t + 2]
+
+
+def early_kernel(earlier_ref, rim_ref, x_ref, early_ref):
     first = (lax.axis_index("z") == 0) & (lax.axis_index("x") == 0)
 
     @pl.when(first)
@@ -94,7 +92,11 @@
 
     @pl.when(jnp.logical_not(first))
     def _():
-        early_ref[...] = earlier_ref[...]
+        for t in range(2):
+            early_ref[t, 0] = rim_ref[t, 0]
+            early_ref[t, 5] = rim_ref[t, 1]
+            for h in range(4):
+                early_ref[t, h + 1] = earlier_ref[t, h]
 
 
 def block_of(early_ref, x_ref):
@@ -312,17 +314,21 @@
     crossing = crossing + [(b, a) for a, b in crossing]
     edge = shape((4, W, CH), bf16)
     own = shape((4, 6, W, CH), bf16)
-    x, inner, outer = call(edge_kernel, [own, edge, edge], [ANY], [dma((3,))])(frames)
+    later = [(i, i + 1) for i in range(shards - 1)]
+    x, inner, outer, late = call(
+        edge_kernel, [own, edge, edge, shape((2, 4, W, CH), bf16)], [ANY], [dma((4,))]
+    )(frames)
+    earlier = lax.ppermute(late, time_axes, later)
     outer = lax.ppermute(outer, row_axes, crossing)
     inner = lax.ppermute(inner, "c", [(0, 1), (1, 0)])
     (codes,) = call(code_kernel, [shape((shards, CH), f32)], [VMEM])(code_grad)
-    x, late = call(
-        late_kernel, [own, shape((2, 6, W, CH), bf16)], [VMEM] * 3 + [ANY], aliases={0: 0}
+    x, rim = call(
+        rim_kernel, [own, shape((2, 2, W, CH), bf16)], [VMEM] * 3 + [ANY], aliases={0: 0}
     )(x, inner, outer, codes)
+    rim = lax.ppermute(rim, time_axes, later)
     codes = lax.all_to_all(codes.reshape(shards, 1, CH), time_axes, 0, 0, tiled=True)
     codes = codes.reshape(shards, CH)
-    earlier = lax.ppermute(late, time_axes, [(i, i + 1) for i in range(shards - 1)])
-    (early,) = call(early_kernel, [shape((2, 6, W, CH), bf16)], [VMEM] * 2)(earlier, x)
+    (early,) = call(early_kernel, [shape((2, 6, W, CH), bf16)], [VMEM] * 3)(earlier, rim, x)
     state, quantized = call(
         forward_kernel,
         [shape((SMALL + 48, CH), f32), shape(centres.shape, f32)],

time: 69.2 us -> 68.4 us (0.988)
  blocking collectives: 32.1 us -> 30.3 us
  starting transfers between devices: 18.5 us -> 19.4 us
    ppermute x1 -> x2, starting transfers between devices: 3.4 us -> 6.51 us  [the longest x1 3.4 us: on_device(): earlier = lax.ppermute(late, time_axes, later)]
    ppermute x1, starting transfers between devices: 2.98 us -> 1.04 us  [on_device(): got = lax.ppermute(theirs, 'c', [(0, 1), (1, 0)])]
    all_to_all x1, blocking collectives: 13 us -> 11.5 us  [on_device(): parts = lax.all_to_all(chunks, 'z', 0, 0, tiled=True)]
  transfers between devices with their start and end apart: 5 -> 6, of which waited for: 2 -> 2; matrix products, arithmetic and copies ran while one was open for 0% -> 0% of each run, Pallas kernels for 8% -> 9%
where the time goes in v4:
time: 68.4 us; the launch traced here: 68 us
  blocking collectives  30.3 us (44%)
  starting transfers between devices  19.4 us (28%)
  Pallas kernels  10.2 us (15%)
  waiting for transfers between devices  5.48 us (8%)
  local copies, waits for them, and re-layouts  1.85 us (3%)
  between operations  0.79 us (1%)
    all_to_all x1, blocking collectives, on_device(): chunks = lax.all_to_all(chunks, ('x', 'y'), 0, 0, tiled=True)  18.8 us
    all_to_all x1, blocking collectives, on_device(): parts = lax.all_to_all(chunks, 'z', 0, 0, tiled=True)  11.5 us
    all_to_all x1, starting transfers between devices, on_device(): lax.all_to_all(codes.reshape(shards, 1, CH), time_axes, 0, 0, tiled=True)  11.1 us
    all_to_all x1, waiting for transfers between devices, on_device(): lax.all_to_all(codes.reshape(shards, 1, CH), time_axes, 0, 0, tiled=True)  4.57 us
    pallas_call x1, Pallas kernels, on_device(): call(forward_kernel, [shape((SMALL + 48, CH), f32), shape(centres.shape,...  3.82 us
    ppermute x1, starting transfers between devices, on_device(): earlier = lax.ppermute(late, time_axes, later)  3.4 us
    pallas_call x1, Pallas kernels, on_device(): call(lambda *refs: backward_kernel(total_cells, *refs), [shape((4, 16, WI...  3.21 us
    ppermute x1, starting transfers between devices, on_device(): rim = lax.ppermute(rim, time_axes, later)  3.11 us
  transfers between devices with their start and end apart: 6, of which 2 were waited for; matrix products, arithmetic and copies ran while one was open for 0% of the time, Pallas kernels for 9%

profile of v4, /device:TPU:2, one launch (start us, length us, event | category | flops | bytes accessed | tf_op | source)
XLA Modules:
  0.0 68.0 jit_solution(21269486314853227)
XLA Ops:
  0.6 0.0 copy-start.1
  0.6 1.0 %copy-done.1 = bf16[4,4,128,128]{3,2,1,0:T(8,128)(2,1)S(1)} copy-done((bf16[4,4,128,128]{3,2,1,0:T(8,128)(2,1)S(1)}, bf16[4,4,128,128]{3,2,1,0:T(8,128)(2,1)}, u32[]{:S(2)}) %copy-start.1) | copy-done | bytes 524312
  1.7 0.0 copy-start
  1.7 0.2 shard_map.102
  1.9 0.1 collective-permute-start.1
  2.0 0.7 collective-permute-start.2
  2.6 3.4 %collective-permute-start = (bf16[2,4,128,128]{3,2,1,0:T(8,128)(2,1)S(1)}, bf16[2,4,128,128]{3,2,1,0:T(8,128)(2,1)S(1)}, u32[]{:S(2)}, u32[]{:S(2)}) collective-permute-start(bf16[2,4,128,128]{3,2,1,0:T(8,128)(2,1)S(1)} %get-tuple-element.18), channel_id=1, source_target_pairs={{0,8},{8,16},{16,24},{24,32},{32,40},{40,48},{48,56},{56,64},{64,7... | collective-permute-start | bytes 786440 | tf_op jit(solution)/shard_map/ppermute | solution.py:321
  6.0 0.0 copy-start.2
  6.1 0.8 %copy-done.2 = f32[32,4,24]{0,2,1:T(8,128)S(1)} copy-done((f32[32,4,24]{0,2,1:T(8,128)S(1)}, f32[32,4,24]{0,2,1:T(8,128)}, u32[]{:S(2)}) %copy-start.2) | copy-done | bytes 12312
  6.8 0.0 copy-start.3
  6.8 0.0 copy-start.4
  6.9 0.0 copy-start.5
  6.9 0.0 copy-start.6
  6.9 0.7 shard_map.103.code_any
  7.5 0.0 collective-permute-done.1.inner_ref
  7.5 0.0 collective-permute-done.2.outer_ref
  7.5 0.1 shard_map.104
  7.6 3.1 %collective-permute-start.3 = (bf16[2,2,128,128]{3,2,1,0:T(8,128)(2,1)S(1)}, bf16[2,2,128,128]{3,2,1,0:T(8,128)(2,1)S(1)}, u32[]{:S(2)}, u32[]{:S(2)}) collective-permute-start(bf16[2,2,128,128]{3,2,1,0:T(8,128)(2,1)S(1)} %get-tuple-element.22), channel_id=1, source_target_pairs={{0,8},{8,16},{16,24},{24,32},{32,40},{40,48},{48,56},{56,64},{64,7... | collective-permute-start | bytes 393224 | tf_op jit(solution)/shard_map/ppermute | solution.py:328
  10.7 11.1 %all-to-all-start = ((f32[32,1,128]{2,1,0:T(1,128)}), f32[32,1,128]{2,1,0:T(1,128)S(1)}, u32[]{:S(2)}, u32[]{:S(2)}) async-start(f32[32,1,128]{2,1,0:T(1,128)} %bitcast.8), calls=%async_computation | async-start | bytes 32768 | tf_op jit(solution)/shard_map/all_to_all | solution.py:329
  21.8 0.0 collective-permute-done.3.rim_ref
  21.8 0.0 collective-permute-done.earlier_ref
  21.9 0.0 copy-done
  21.9 0.0 copy-done.3
  21.9 0.0 copy-done.4
  21.9 0.0 copy-done.5
  21.9 0.0 copy-done.6
  21.9 3.8 %shard_map.106 = (f32[2608,128]{1,0:T(8,128)S(1)}, f32[4,24,32]{2,1,0:T(8,128)}) custom-call(s32[1,6]{1,0:T(1,128)S(1)} %bitcast.19, s32[4,24,32]{2,1,0:T(8,128)S(1)} %bitcast.17, bf16[2,6,128,128]{3,2,1,0:T(8,128)(2,1)S(1)} %shard_map.105.early_ref.refs_0_, bf16[4,6,128,128]{3,2,1,0:T(8,128)(2,1)S(1)} %get-tuple-element.23.x_ref.refs_1_, ...), custom_call_target="tpu_custom_call" | custom-call | tf_op jit(solution)/shard_map/pallas_call | solution.py:332
  25.8 4.6 %all-to-all-done = f32[32,1,128]{2,1,0:T(1,128)S(1)} async-done(((f32[32,1,128]{2,1,0:T(1,128)}), f32[32,1,128]{2,1,0:T(1,128)S(1)}, u32[]{:S(2)}, u32[]{:S(2)}) %all-to-all-start) | async-done | bytes 16416 | tf_op jit(solution)/shard_map/all_to_all | solution.py:329
  30.3 3.2 %shard_map.107 = (f32[4,16,3584]{2,1,0:T(8,128)S(1)}, bf16[384,2048]{1,0:T(8,128)(2,1)S(1)}, f32[8,128]{1,0:T(8,128)S(1)}) custom-call(bf16[2,6,128,128]{3,2,1,0:T(8,128)(2,1)S(1)} %shard_map.105.early_ref.refs_0_, bf16[4,6,128,128]{3,2,1,0:T(8,128)(2,1)S(1)} %get-tuple-element.23.x_ref.refs_1_, f32[2608,128]{1,0:T(8,128)S(1)} %get-tuple-element.25.refs_2_, ...), custom_call_target="tpu_custom_call" | custom-call | tf_op jit(solution)/shard_map/pallas_call | solution.py:347
  33.5 1.0 %collective-permute-start.4 = (f32[4,16,3584]{2,1,0:T(8,128)S(1)}, f32[4,16,3584]{2,1,0:T(8,128)S(1)}, u32[]{:S(2)}, u32[]{:S(2)}) collective-permute-start(f32[4,16,3584]{2,1,0:T(8,128)S(1)} %get-tuple-element.28), channel_id=1, source_target_pairs={{0,1},{1,0},{2,3},{3,2},{4,5},{5,4},{6,7},{7,6},{8,9},{9,8},{10,11... | collective-permute-start | bytes 2752520 | tf_op jit(solution)/shard_map/ppermute | solution.py:353
  34.6 1.2 %shard_map.108.mine_ref = f32[4,16,3584]{2,1,0:T(8,128)S(1)} custom-call(bf16[2,6,128,128]{3,2,1,0:T(8,128)(2,1)S(1)} %shard_map.105.early_ref.refs_0_, bf16[4,6,128,128]{3,2,1,0:T(8,128)(2,1)S(1)} %get-tuple-element.23.x_ref.refs_1_, bf16[384,2048]{1,0:T(8,128)(2,1)S(1)} %get-tuple-element.26.low_ref, f32[8,128]{1,0:T(8,128)S(1)} %get-tuple-element.27.small_ref), custom_call_target="tpu_custom_call" | custom-call | tf_op jit(solution)/shard_map/pallas_call | solution.py:354
  35.8 0.9 %collective-permute-done.4.got_ref = f32[4,16,3584]{2,1,0:T(8,128)S(1)} collective-permute-done((f32[4,16,3584]{2,1,0:T(8,128)S(1)}, f32[4,16,3584]{2,1,0:T(8,128)S(1)}, u32[]{:S(2)}, u32[]{:S(2)}) %collective-permute-start.4) | collective-permute-done | bytes 917536 | tf_op jit(solution)/shard_map/ppermute | solution.py:353
  36.7 0.3 shard_map.109
  37.0 18.8 %all_to_all.15.parts_ref = bf16[16,144,128]{2,1,0:T(8,128)(2,1)S(1)} all-to-all(bf16[16,144,128]{2,1,0:T(8,128)(2,1)S(1)} %shard_map.109), channel_id=1, replica_groups=mesh['z'=8,'x'=4,'y'=4,'c'=2] {'x','y'}, dimensions={0} | all-to-all | bytes 1179648 | tf_op jit(solution)/shard_map/all_to_all | solution.py:356
  55.9 0.1 shard_map.110
  55.9 11.5 %all_to_all.16.parts_ref = f32[8,24,128]{2,1,0:T(8,128)S(1)} all-to-all(f32[8,24,128]{2,1,0:T(8,128)S(1)} %shard_map.110), channel_id=1, replica_groups=mesh['z'=8,'x'=4,'y'=4,'c'=2] {'z'}, dimensions={0} | all-to-all | bytes 196608 | tf_op jit(solution)/shard_map/all_to_all | solution.py:358
  67.4 0.6 shard_map.111
  (1 shorter events, 0.0 us)
Async XLA Ops:
  0.6 1.0 %copy-start.1 = (bf16[4,4,128,128]{3,2,1,0:T(8,128)(2,1)S(1)}, bf16[4,4,128,128]{3,2,1,0:T(8,128)(2,1)}, u32[]{:S(2)}) copy-start(bf16[4,4,128,128]{3,2,1,0:T(8,128)(2,1)} %frames_any.1) | copy-start | bytes 1572868
  1.7 20.2 %copy-start = (bf16[3456,128]{1,0:T(8,128)(2,1)S(1)}, bf16[3456,128]{1,0:T(8,128)(2,1)}, u32[]{:S(2)}) copy-start(bf16[3456,128]{1,0:T(8,128)(2,1)} %param.8) | copy-start | bytes 2654212
  1.9 5.7 %collective-permute-start.1 = (bf16[4,128,128]{2,1,0:T(8,128)(2,1)S(1)}, bf16[4,128,128]{2,1,0:T(8,128)(2,1)S(1)}, u32[]{:S(2)}, u32[]{:S(2)}) collective-permute-start(bf16[4,128,128]{2,1,0:T(8,128)(2,1)S(1)} %get-tuple-element.20), channel_id=1, source_target_pairs={{0,1},{1,0},{2,3},{3,2},{4,5},{5,4},{6,7},{7,6},{8,9},{9,8},{10,11... | collective-permute-start | bytes 393224 | tf_op jit(solution)/shard_map/ppermute | solution.py:323
  2.0 5.6 %collective-permute-start.2 = (bf16[4,128,128]{2,1,0:T(8,128)(2,1)S(1)}, bf16[4,128,128]{2,1,0:T(8,128)(2,1)S(1)}, u32[]{:S(2)}, u32[]{:S(2)}) collective-permute-start(bf16[4,128,128]{2,1,0:T(8,128)(2,1)S(1)} %get-tuple-element.21), channel_id=1, source_target_pairs={{1,2},{3,4},{5,6},{2,1},{4,3},{6,5},{9,10},{11,12},{13,14},{10,9},... | collective-permute-start | bytes 393224 | tf_op jit(solution)/shard_map/ppermute | solution.py:322
  2.6 19.2 %collective-permute-start = (bf16[2,4,128,128]{3,2,1,0:T(8,128)(2,1)S(1)}, bf16[2,4,128,128]{3,2,1,0:T(8,128)(2,1)S(1)}, u32[]{:S(2)}, u32[]{:S(2)}) collective-permute-start(bf16[2,4,128,128]{3,2,1,0:T(8,128)(2,1)S(1)} %get-tuple-element.18), channel_id=1, source_target_pairs={{0,8},{8,16},{16,24},{24,32},{32,40},{40,48},{48,56},{56,64},{64,7... | collective-permute-start | bytes 786440 | tf_op jit(solution)/shard_map/ppermute | solution.py:321
  6.0 0.8 %copy-start.2 = (f32[32,4,24]{0,2,1:T(8,128)S(1)}, f32[32,4,24]{0,2,1:T(8,128)}, u32[]{:S(2)}) copy-start(f32[32,4,24]{0,2,1:T(8,128)} %param.13) | copy-start | bytes 36868
  6.8 15.1 %copy-start.3 = (s32[32,4,24]{0,2,1:T(8,128)S(1)}, s32[32,4,24]{0,2,1:T(8,128)}, u32[]{:S(2)}) copy-start(s32[32,4,24]{0,2,1:T(8,128)} %param.12) | copy-start | bytes 36868
  6.8 15.1 %copy-start.4 = (f32[128,6]{0,1:T(8,128)S(1)}, f32[128,6]{0,1:T(8,128)}, u32[]{:S(2)}) copy-start(f32[128,6]{0,1:T(8,128)} %param.10) | copy-start | bytes 9220
  6.9 15.1 %copy-start.5 = (s32[6]{0:T(128)S(1)}, s32[6]{0:T(128)}, u32[]{:S(2)}) copy-start(s32[6]{0:T(128)} %param.11) | copy-start | bytes 76
  6.9 15.1 %copy-start.6 = (f32[128]{0:T(128)S(1)}, f32[128]{0:T(128)}, u32[]{:S(2)}) copy-start(f32[128]{0:T(128)} %param.9) | copy-start | bytes 1540
  7.6 14.2 %collective-permute-start.3 = (bf16[2,2,128,128]{3,2,1,0:T(8,128)(2,1)S(1)}, bf16[2,2,128,128]{3,2,1,0:T(8,128)(2,1)S(1)}, u32[]{:S(2)}, u32[]{:S(2)}) collective-permute-start(bf16[2,2,128,128]{3,2,1,0:T(8,128)(2,1)S(1)} %get-tuple-element.22), channel_id=1, source_target_pairs={{0,8},{8,16},{16,24},{24,32},{32,40},{40,48},{48,56},{56,64},{64,7... | collective-permute-start | bytes 393224 | tf_op jit(solution)/shard_map/ppermute | solution.py:328
  10.7 19.6 %all-to-all-start = ((f32[32,1,128]{2,1,0:T(1,128)}), f32[32,1,128]{2,1,0:T(1,128)S(1)}, u32[]{:S(2)}, u32[]{:S(2)}) async-start(f32[32,1,128]{2,1,0:T(1,128)} %bitcast.8), calls=%async_computation | async-start | bytes 32768 | tf_op jit(solution)/shard_map/all_to_all | solution.py:329
  33.5 3.1 %collective-permute-start.4 = (f32[4,16,3584]{2,1,0:T(8,128)S(1)}, f32[4,16,3584]{2,1,0:T(8,128)S(1)}, u32[]{:S(2)}, u32[]{:S(2)}) collective-permute-start(f32[4,16,3584]{2,1,0:T(8,128)S(1)} %get-tuple-element.28), channel_id=1, source_target_pairs={{0,1},{1,0},{2,3},{3,2},{4,5},{5,4},{6,7},{7,6},{8,9},{9,8},{10,11... | collective-permute-start | bytes 2752520 | tf_op jit(solution)/shard_map/ppermute | solution.py:353

commit v5 on v4

--- a/solution.py
+++ b/solution.py
@@ -270,25 +270,29 @@
     small = jnp.concatenate([high, small - high], 0).astype(bf16)
     share = LANES // 32
     for y in range(4):
-        for k in range(32):
-            start = k * share
-            base = start // CH * CH
-            window = mine_ref[y, :, base : base + 2 * CH] + got_ref[y, :, base : base + 2 * CH]
-            if start > base:
-                window = pltpu.roll(window, 2 * CH - (start - base), 1)
-            z, x = divmod(k, 4)
-            out_ref[x * 4 + y, z * 16 : (z + 1) * 16] = window[:, :CH].astype(bf16)
+        total = mine_ref[y, :, :LANES] + got_ref[y, :, :LANES]
         for x in range(4):
-            out_ref[x * 4 + y, 128:144] = small
+            pieces = [
+                total[:, (4 * z + x) * share : (4 * z + x + 1) * share] for z in range(8)
+            ]
+            dense = jnp.concatenate(pieces + [jnp.zeros((16, 7 * CH - 8 * share), f32)], 1)
+            out_ref[x * 4 + y, :, : 7 * CH] = dense.astype(bf16)
+            out_ref[x * 4 + y, :, 7 * CH :] = small
 
 
 def plane_kernel(parts_ref, out_ref):
     total = parts_ref[0].astype(f32)
     for k in range(1, parts_ref.shape[0]):
         total = total + parts_ref[k].astype(f32)
-    small = total[128:136] + total[136:144]
+    small = total[0:8, 7 * CH :] + total[8:16, 7 * CH :]
+    share = LANES // 32
     for z in range(8):
-        out_ref[z, 0:16] = total[z * 16 : (z + 1) * 16]
+        start = z * share
+        base = start // CH * CH
+        window = total[:, base : base + 2 * CH]
+        if start > base:
+            window = pltpu.roll(window, 2 * CH - (start - base), 1)
+        out_ref[z, 0:16] = window[:, :CH]
         out_ref[z, 16:24] = small
 
 
@@ -352,7 +356,7 @@
 
     got = lax.ppermute(theirs, "c", [(0, 1), (1, 0)])
     (mine,) = call(own_kernel, [shape((4, 16, WIDE), f32)], [VMEM] * 4)(early, x, low, small)
-    (chunks,) = call(pair_kernel, [shape((16, 144, CH), bf16)], [VMEM] * 2)(mine, got)
+    (chunks,) = call(pair_kernel, [shape((16, 16, 8 * CH), bf16)], [VMEM] * 2)(mine, got)
     chunks = lax.all_to_all(chunks, ("x", "y"), 0, 0, tiled=True)
     (chunks,) = call(plane_kernel, [shape((8, 24, CH), f32)], [VMEM])(chunks)
     parts = lax.all_to_all(chunks, "z", 0, 0, tiled=True)

time: 68.4 us -> 67.7 us (0.990); the launches traced: 68 us -> 66.5 us
  blocking collectives: 30.3 us -> 28.7 us
    all_to_all x1, blocking collectives: 18.8 us -> 17.2 us  [on_device(): chunks = lax.all_to_all(chunks, ('x', 'y'), 0, 0, tiled=True)]
where the time goes in v5:
time: 67.7 us; the launch traced here: 66.5 us
  blocking collectives  28.7 us (42%)
  starting transfers between devices  19.4 us (29%)
  Pallas kernels  10.2 us (15%)
  waiting for transfers between devices  5.48 us (8%)
  local copies, waits for them, and re-layouts  1.85 us (3%)
  between operations  0.79 us (1%)
    all_to_all x1, blocking collectives, on_device(): chunks = lax.all_to_all(chunks, ('x', 'y'), 0, 0, tiled=True)  17.2 us
    all_to_all x1, blocking collectives, on_device(): parts = lax.all_to_all(chunks, 'z', 0, 0, tiled=True)  11.5 us
    all_to_all x1, starting transfers between devices, on_device(): lax.all_to_all(codes.reshape(shards, 1, CH), time_axes, 0, 0, tiled=True)  11.1 us
    all_to_all x1, waiting for transfers between devices, on_device(): lax.all_to_all(codes.reshape(shards, 1, CH), time_axes, 0, 0, tiled=True)  4.57 us
    pallas_call x1, Pallas kernels, on_device(): call(forward_kernel, [shape((SMALL + 48, CH), f32), shape(centres.shape,...  3.82 us
    ppermute x1, starting transfers between devices, on_device(): earlier = lax.ppermute(late, time_axes, later)  3.4 us
    pallas_call x1, Pallas kernels, on_device(): call(lambda *refs: backward_kernel(total_cells, *refs), [shape((4, 16, WI...  3.21 us
    ppermute x1, starting transfers between devices, on_device(): rim = lax.ppermute(rim, time_axes, later)  3.11 us
  transfers between devices with their start and end apart: 6, of which 2 were waited for; matrix products, arithmetic and copies ran while one was open for 0% of the time, Pallas kernels for 9%

profile of v5, /device:TPU:2, one launch (start us, length us, event | category | flops | bytes accessed | tf_op | source)
XLA Modules:
  0.0 66.5 jit_solution(7504996233475846119)
XLA Ops:
  0.6 0.0 copy-start.1
  0.6 1.0 %copy-done.1 = bf16[4,4,128,128]{3,2,1,0:T(8,128)(2,1)S(1)} copy-done((bf16[4,4,128,128]{3,2,1,0:T(8,128)(2,1)S(1)}, bf16[4,4,128,128]{3,2,1,0:T(8,128)(2,1)}, u32[]{:S(2)}) %copy-start.1) | copy-done | bytes 524312
  1.7 0.0 copy-start
  1.7 0.2 shard_map.102
  1.9 0.1 collective-permute-start.1
  2.0 0.7 %collective-permute-start.2 = (bf16[4,128,128]{2,1,0:T(8,128)(2,1)S(1)}, bf16[4,128,128]{2,1,0:T(8,128)(2,1)S(1)}, u32[]{:S(2)}, u32[]{:S(2)}) collective-permute-start(bf16[4,128,128]{2,1,0:T(8,128)(2,1)S(1)} %get-tuple-element.21), channel_id=1, source_target_pairs={{1,2},{3,4},{5,6},{2,1},{4,3},{6,5},{9,10},{11,12},{13,14},{10,9},... | collective-permute-start | bytes 393224 | tf_op jit(solution)/shard_map/ppermute | solution.py:326
  2.6 3.4 %collective-permute-start = (bf16[2,4,128,128]{3,2,1,0:T(8,128)(2,1)S(1)}, bf16[2,4,128,128]{3,2,1,0:T(8,128)(2,1)S(1)}, u32[]{:S(2)}, u32[]{:S(2)}) collective-permute-start(bf16[2,4,128,128]{3,2,1,0:T(8,128)(2,1)S(1)} %get-tuple-element.18), channel_id=1, source_target_pairs={{0,8},{8,16},{16,24},{24,32},{32,40},{40,48},{48,56},{56,64},{64,7... | collective-permute-start | bytes 786440 | tf_op jit(solution)/shard_map/ppermute | solution.py:325
  6.0 0.0 copy-start.2
  6.1 0.8 %copy-done.2 = f32[32,4,24]{0,2,1:T(8,128)S(1)} copy-done((f32[32,4,24]{0,2,1:T(8,128)S(1)}, f32[32,4,24]{0,2,1:T(8,128)}, u32[]{:S(2)}) %copy-start.2) | copy-done | bytes 12312
  6.8 0.0 copy-start.3
  6.8 0.0 copy-start.4
  6.9 0.0 copy-start.5
  6.9 0.0 copy-start.6
  6.9 0.7 %shard_map.103.code_any = f32[32,128]{1,0:T(8,128)} custom-call(f32[4,24,32]{2,1,0:T(8,128)S(1)} %bitcast.16), custom_call_target="tpu_custom_call" | custom-call | tf_op jit(solution)/shard_map/pallas_call | solution.py:328
  7.5 0.0 collective-permute-done.1.inner_ref
  7.5 0.0 collective-permute-done.2.outer_ref
  7.5 0.1 shard_map.104
  7.6 3.1 %collective-permute-start.3 = (bf16[2,2,128,128]{3,2,1,0:T(8,128)(2,1)S(1)}, bf16[2,2,128,128]{3,2,1,0:T(8,128)(2,1)S(1)}, u32[]{:S(2)}, u32[]{:S(2)}) collective-permute-start(bf16[2,2,128,128]{3,2,1,0:T(8,128)(2,1)S(1)} %get-tuple-element.22), channel_id=1, source_target_pairs={{0,8},{8,16},{16,24},{24,32},{32,40},{40,48},{48,56},{56,64},{64,7... | collective-permute-start | bytes 393224 | tf_op jit(solution)/shard_map/ppermute | solution.py:332
  10.7 11.1 %all-to-all-start = ((f32[32,1,128]{2,1,0:T(1,128)}), f32[32,1,128]{2,1,0:T(1,128)S(1)}, u32[]{:S(2)}, u32[]{:S(2)}) async-start(f32[32,1,128]{2,1,0:T(1,128)} %bitcast.8), calls=%async_computation | async-start | bytes 32768 | tf_op jit(solution)/shard_map/all_to_all | solution.py:333
  21.8 0.0 collective-permute-done.3.rim_ref
  21.8 0.0 collective-permute-done.earlier_ref
  21.9 0.0 copy-done
  21.9 0.0 copy-done.3
  21.9 0.0 copy-done.4
  21.9 0.0 copy-done.5
  21.9 0.0 copy-done.6
  21.9 3.8 %shard_map.106 = (f32[2608,128]{1,0:T(8,128)S(1)}, f32[4,24,32]{2,1,0:T(8,128)}) custom-call(s32[1,6]{1,0:T(1,128)S(1)} %bitcast.19, s32[4,24,32]{2,1,0:T(8,128)S(1)} %bitcast.17, bf16[2,6,128,128]{3,2,1,0:T(8,128)(2,1)S(1)} %shard_map.105.early_ref.refs_0_, bf16[4,6,128,128]{3,2,1,0:T(8,128)(2,1)S(1)} %get-tuple-element.23.x_ref.refs_1_, ...), custom_call_target="tpu_custom_call" | custom-call | tf_op jit(solution)/shard_map/pallas_call | solution.py:336
  25.8 4.6 %all-to-all-done = f32[32,1,128]{2,1,0:T(1,128)S(1)} async-done(((f32[32,1,128]{2,1,0:T(1,128)}), f32[32,1,128]{2,1,0:T(1,128)S(1)}, u32[]{:S(2)}, u32[]{:S(2)}) %all-to-all-start) | async-done | bytes 16416 | tf_op jit(solution)/shard_map/all_to_all | solution.py:333
  30.3 3.2 %shard_map.107 = (f32[4,16,3584]{2,1,0:T(8,128)S(1)}, bf16[384,2048]{1,0:T(8,128)(2,1)S(1)}, f32[8,128]{1,0:T(8,128)S(1)}) custom-call(bf16[2,6,128,128]{3,2,1,0:T(8,128)(2,1)S(1)} %shard_map.105.early_ref.refs_0_, bf16[4,6,128,128]{3,2,1,0:T(8,128)(2,1)S(1)} %get-tuple-element.23.x_ref.refs_1_, f32[2608,128]{1,0:T(8,128)S(1)} %get-tuple-element.25.refs_2_, ...), custom_call_target="tpu_custom_call" | custom-call | tf_op jit(solution)/shard_map/pallas_call | solution.py:351
  33.5 1.0 %collective-permute-start.4 = (f32[4,16,3584]{2,1,0:T(8,128)S(1)}, f32[4,16,3584]{2,1,0:T(8,128)S(1)}, u32[]{:S(2)}, u32[]{:S(2)}) collective-permute-start(f32[4,16,3584]{2,1,0:T(8,128)S(1)} %get-tuple-element.28), channel_id=1, source_target_pairs={{0,1},{1,0},{2,3},{3,2},{4,5},{5,4},{6,7},{7,6},{8,9},{9,8},{10,11... | collective-permute-start | bytes 2752520 | tf_op jit(solution)/shard_map/ppermute | solution.py:357
  34.6 1.2 %shard_map.108.mine_ref = f32[4,16,3584]{2,1,0:T(8,128)S(1)} custom-call(bf16[2,6,128,128]{3,2,1,0:T(8,128)(2,1)S(1)} %shard_map.105.early_ref.refs_0_, bf16[4,6,128,128]{3,2,1,0:T(8,128)(2,1)S(1)} %get-tuple-element.23.x_ref.refs_1_, bf16[384,2048]{1,0:T(8,128)(2,1)S(1)} %get-tuple-element.26.low_ref, f32[8,128]{1,0:T(8,128)S(1)} %get-tuple-element.27.small_ref), custom_call_target="tpu_custom_call" | custom-call | tf_op jit(solution)/shard_map/pallas_call | solution.py:358
  35.8 0.9 %collective-permute-done.4.got_ref = f32[4,16,3584]{2,1,0:T(8,128)S(1)} collective-permute-done((f32[4,16,3584]{2,1,0:T(8,128)S(1)}, f32[4,16,3584]{2,1,0:T(8,128)S(1)}, u32[]{:S(2)}, u32[]{:S(2)}) %collective-permute-start.4) | collective-permute-done | bytes 917536 | tf_op jit(solution)/shard_map/ppermute | solution.py:357
  36.7 0.3 shard_map.109
  37.0 17.2 %all_to_all.15.parts_ref = bf16[16,16,1024]{2,1,0:T(8,128)(2,1)S(1)} all-to-all(bf16[16,16,1024]{2,1,0:T(8,128)(2,1)S(1)} %shard_map.109), channel_id=1, replica_groups=mesh['z'=8,'x'=4,'y'=4,'c'=2] {'x','y'}, dimensions={0} | all-to-all | bytes 1048576 | tf_op jit(solution)/shard_map/all_to_all | solution.py:360
  54.2 0.1 shard_map.110
  54.4 11.5 %all_to_all.16.parts_ref = f32[8,24,128]{2,1,0:T(8,128)S(1)} all-to-all(f32[8,24,128]{2,1,0:T(8,128)S(1)} %shard_map.110), channel_id=1, replica_groups=mesh['z'=8,'x'=4,'y'=4,'c'=2] {'z'}, dimensions={0} | all-to-all | bytes 196608 | tf_op jit(solution)/shard_map/all_to_all | solution.py:362
  65.8 0.6 shard_map.111
  (1 shorter events, 0.0 us)
Async XLA Ops:
  0.6 1.0 %copy-start.1 = (bf16[4,4,128,128]{3,2,1,0:T(8,128)(2,1)S(1)}, bf16[4,4,128,128]{3,2,1,0:T(8,128)(2,1)}, u32[]{:S(2)}) copy-start(bf16[4,4,128,128]{3,2,1,0:T(8,128)(2,1)} %frames_any.1) | copy-start | bytes 1572868
  1.7 20.2 %copy-start = (bf16[3456,128]{1,0:T(8,128)(2,1)S(1)}, bf16[3456,128]{1,0:T(8,128)(2,1)}, u32[]{:S(2)}) copy-start(bf16[3456,128]{1,0:T(8,128)(2,1)} %param.8) | copy-start | bytes 2654212
  1.9 5.7 %collective-permute-start.1 = (bf16[4,128,128]{2,1,0:T(8,128)(2,1)S(1)}, bf16[4,128,128]{2,1,0:T(8,128)(2,1)S(1)}, u32[]{:S(2)}, u32[]{:S(2)}) collective-permute-start(bf16[4,128,128]{2,1,0:T(8,128)(2,1)S(1)} %get-tuple-element.20), channel_id=1, source_target_pairs={{0,1},{1,0},{2,3},{3,2},{4,5},{5,4},{6,7},{7,6},{8,9},{9,8},{10,11... | collective-permute-start | bytes 393224 | tf_op jit(solution)/shard_map/ppermute | solution.py:327
  2.0 5.6 %collective-permute-start.2 = (bf16[4,128,128]{2,1,0:T(8,128)(2,1)S(1)}, bf16[4,128,128]{2,1,0:T(8,128)(2,1)S(1)}, u32[]{:S(2)}, u32[]{:S(2)}) collective-permute-start(bf16[4,128,128]{2,1,0:T(8,128)(2,1)S(1)} %get-tuple-element.21), channel_id=1, source_target_pairs={{1,2},{3,4},{5,6},{2,1},{4,3},{6,5},{9,10},{11,12},{13,14},{10,9},... | collective-permute-start | bytes 393224 | tf_op jit(solution)/shard_map/ppermute | solution.py:326
  2.6 19.2 %collective-permute-start = (bf16[2,4,128,128]{3,2,1,0:T(8,128)(2,1)S(1)}, bf16[2,4,128,128]{3,2,1,0:T(8,128)(2,1)S(1)}, u32[]{:S(2)}, u32[]{:S(2)}) collective-permute-start(bf16[2,4,128,128]{3,2,1,0:T(8,128)(2,1)S(1)} %get-tuple-element.18), channel_id=1, source_target_pairs={{0,8},{8,16},{16,24},{24,32},{32,40},{40,48},{48,56},{56,64},{64,7... | collective-permute-start | bytes 786440 | tf_op jit(solution)/shard_map/ppermute | solution.py:325
  6.0 0.8 %copy-start.2 = (f32[32,4,24]{0,2,1:T(8,128)S(1)}, f32[32,4,24]{0,2,1:T(8,128)}, u32[]{:S(2)}) copy-start(f32[32,4,24]{0,2,1:T(8,128)} %param.13) | copy-start | bytes 36868
  6.8 15.1 %copy-start.3 = (s32[32,4,24]{0,2,1:T(8,128)S(1)}, s32[32,4,24]{0,2,1:T(8,128)}, u32[]{:S(2)}) copy-start(s32[32,4,24]{0,2,1:T(8,128)} %param.12) | copy-start | bytes 36868
  6.8 15.1 %copy-start.4 = (f32[128,6]{0,1:T(8,128)S(1)}, f32[128,6]{0,1:T(8,128)}, u32[]{:S(2)}) copy-start(f32[128,6]{0,1:T(8,128)} %param.10) | copy-start | bytes 9220
  6.9 15.1 %copy-start.5 = (s32[6]{0:T(128)S(1)}, s32[6]{0:T(128)}, u32[]{:S(2)}) copy-start(s32[6]{0:T(128)} %param.11) | copy-start | bytes 76
  6.9 15.1 %copy-start.6 = (f32[128]{0:T(128)S(1)}, f32[128]{0:T(128)}, u32[]{:S(2)}) copy-start(f32[128]{0:T(128)} %param.9) | copy-start | bytes 1540
  7.6 14.2 %collective-permute-start.3 = (bf16[2,2,128,128]{3,2,1,0:T(8,128)(2,1)S(1)}, bf16[2,2,128,128]{3,2,1,0:T(8,128)(2,1)S(1)}, u32[]{:S(2)}, u32[]{:S(2)}) collective-permute-start(bf16[2,2,128,128]{3,2,1,0:T(8,128)(2,1)S(1)} %get-tuple-element.22), channel_id=1, source_target_pairs={{0,8},{8,16},{16,24},{24,32},{32,40},{40,48},{48,56},{56,64},{64,7... | collective-permute-start | bytes 393224 | tf_op jit(solution)/shard_map/ppermute | solution.py:332
  10.7 19.6 %all-to-all-start = ((f32[32,1,128]{2,1,0:T(1,128)}), f32[32,1,128]{2,1,0:T(1,128)S(1)}, u32[]{:S(2)}, u32[]{:S(2)}) async-start(f32[32,1,128]{2,1,0:T(1,128)} %bitcast.8), calls=%async_computation | async-start | bytes 32768 | tf_op jit(solution)/shard_map/all_to_all | solution.py:333
  33.5 3.1 %collective-permute-start.4 = (f32[4,16,3584]{2,1,0:T(8,128)S(1)}, f32[4,16,3584]{2,1,0:T(8,128)S(1)}, u32[]{:S(2)}, u32[]{:S(2)}) collective-permute-start(f32[4,16,3584]{2,1,0:T(8,128)S(1)} %get-tuple-element.28), channel_id=1, source_target_pairs={{0,1},{1,0},{2,3},{3,2},{4,5},{5,4},{6,7},{7,6},{8,9},{9,8},{10,11... | collective-permute-start | bytes 2752520 | tf_op jit(solution)/shard_map/ppermute | solution.py:357

commit v6 on v5

--- a/solution.py
+++ b/solution.py
@@ -234,11 +234,16 @@
     bias_row = bias_part.sum(0, keepdims=True)
     row = lax.broadcasted_iota(jnp.int32, (8, CH), 0)
     small = jnp.where(row == L, bias_row, projection_part)
-    small_ref[...] = small
+    pieces = split_small(small)
+    small_ref[...] = pieces[0:8].astype(f32) + pieces[8:16].astype(f32)
     kernel_gradient(1 - core, early_ref, x_ref, low_ref, theirs_ref)
     for y in range(4):
-        theirs_ref[y, 0:8, LANES:] = small
-        theirs_ref[y, 8:16, LANES:] = jnp.zeros((8, CH), f32)
+        theirs_ref[y, :, LANES:] = pieces
+
+
+def split_small(small):
+    high = small.astype(bf16).astype(f32)
+    return jnp.concatenate([high, small - high], 0).astype(bf16)
 
 
 def kernel_gradient(core, early_ref, x_ref, low_ref, out_ref):
@@ -254,7 +259,8 @@
                 to = slice((3 * (start + place) + c) * CH, (3 * (start + place) + c + 1) * CH)
                 for y in range(4):
                     row = (c * 4 + y) * 16
-                    out_ref[y, :, to] = result[row : row + 16, place * CH : (place + 1) * CH]
+                    part = result[row : row + 16, place * CH : (place + 1) * CH]
+                    out_ref[y, :, to] = part.astype(out_ref.dtype)
 
 
 def own_kernel(early_ref, x_ref, low_ref, small_ref, mine_ref):
@@ -265,12 +271,11 @@
 
 
 def pair_kernel(mine_ref, got_ref, out_ref):
-    small = mine_ref[0, 0:8, LANES:] + got_ref[0, 0:8, LANES:]
-    high = small.astype(bf16).astype(f32)
-    small = jnp.concatenate([high, small - high], 0).astype(bf16)
+    got_small = got_ref[0, :, LANES:].astype(f32)
+    small = split_small(mine_ref[0, 0:8, LANES:] + (got_small[0:8] + got_small[8:16]))
     share = LANES // 32
     for y in range(4):
-        total = mine_ref[y, :, :LANES] + got_ref[y, :, :LANES]
+        total = mine_ref[y, :, :LANES] + got_ref[y, :, :LANES].astype(f32)
         for x in range(4):
             pieces = [
                 total[:, (4 * z + x) * share : (4 * z + x + 1) * share] for z in range(8)
@@ -350,7 +355,7 @@
     total_cells = 4 * shards * 4 * strips * W
     theirs, low, small = call(
         lambda *refs: backward_kernel(total_cells, *refs),
-        [shape((4, 16, WIDE), f32), shape((3 * CH, 16 * W), bf16), shape((8, CH), f32)],
+        [shape((4, 16, WIDE), bf16), shape((3 * CH, 16 * W), bf16), shape((8, CH), f32)],
         [VMEM] * 4,
     )(early, x, state, codes)
 

time: 67.7 us -> 67 us (0.990)
  no operation moved by 1% of the time
where the time goes in v6:
time: 67 us; the launch traced here: 65.8 us
  blocking collectives  28.7 us (43%)
  starting transfers between devices  19.4 us (29%)
  Pallas kernels  10.2 us (15%)
  waiting for transfers between devices  4.82 us (7%)
  local copies, waits for them, and re-layouts  1.85 us (3%)
  between operations  0.79 us (1%)
    all_to_all x1, blocking collectives, on_device(): chunks = lax.all_to_all(chunks, ('x', 'y'), 0, 0, tiled=True)  17.2 us
    all_to_all x1, blocking collectives, on_device(): parts = lax.all_to_all(chunks, 'z', 0, 0, tiled=True)  11.5 us
    all_to_all x1, starting transfers between devices, on_device(): lax.all_to_all(codes.reshape(shards, 1, CH), time_axes, 0, 0, tiled=True)  11.1 us
    all_to_all x1, waiting for transfers between devices, on_device(): lax.all_to_all(codes.reshape(shards, 1, CH), time_axes, 0, 0, tiled=True)  4.57 us
    pallas_call x1, Pallas kernels, on_device(): call(forward_kernel, [shape((SMALL + 48, CH), f32), shape(centres.shape,...  3.82 us
    ppermute x1, starting transfers between devices, on_device(): earlier = lax.ppermute(late, time_axes, later)  3.4 us
    pallas_call x1, Pallas kernels, on_device(): call(lambda *refs: backward_kernel(total_cells, *refs), [shape((4, 16, WI...  3.21 us
    ppermute x1, starting transfers between devices, on_device(): rim = lax.ppermute(rim, time_axes, later)  3.11 us
  transfers between devices with their start and end apart: 6, of which 2 were waited for; matrix products, arithmetic and copies ran while one was open for 0% of the time, Pallas kernels for 9%

profile of v6, /device:TPU:2, one launch (start us, length us, event | category | flops | bytes accessed | tf_op | source)
XLA Modules:
  0.0 65.8 jit_solution(18085963144570718621)
XLA Ops:
  0.6 0.0 copy-start.1
  0.6 1.0 %copy-done.1 = bf16[4,4,128,128]{3,2,1,0:T(8,128)(2,1)S(1)} copy-done((bf16[4,4,128,128]{3,2,1,0:T(8,128)(2,1)S(1)}, bf16[4,4,128,128]{3,2,1,0:T(8,128)(2,1)}, u32[]{:S(2)}) %copy-start.1) | copy-done | bytes 524312
  1.7 0.0 copy-start
  1.7 0.2 shard_map.102
  1.9 0.1 collective-permute-start.1
  2.0 0.7 %collective-permute-start.2 = (bf16[4,128,128]{2,1,0:T(8,128)(2,1)S(1)}, bf16[4,128,128]{2,1,0:T(8,128)(2,1)S(1)}, u32[]{:S(2)}, u32[]{:S(2)}) collective-permute-start(bf16[4,128,128]{2,1,0:T(8,128)(2,1)S(1)} %get-tuple-element.21), channel_id=1, source_target_pairs={{1,2},{3,4},{5,6},{2,1},{4,3},{6,5},{9,10},{11,12},{13,14},{10,9},... | collective-permute-start | bytes 393224 | tf_op jit(solution)/shard_map/ppermute | solution.py:331
  2.6 3.4 %collective-permute-start = (bf16[2,4,128,128]{3,2,1,0:T(8,128)(2,1)S(1)}, bf16[2,4,128,128]{3,2,1,0:T(8,128)(2,1)S(1)}, u32[]{:S(2)}, u32[]{:S(2)}) collective-permute-start(bf16[2,4,128,128]{3,2,1,0:T(8,128)(2,1)S(1)} %get-tuple-element.18), channel_id=1, source_target_pairs={{0,8},{8,16},{16,24},{24,32},{32,40},{40,48},{48,56},{56,64},{64,7... | collective-permute-start | bytes 786440 | tf_op jit(solution)/shard_map/ppermute | solution.py:330
  6.0 0.0 copy-start.2
  6.1 0.8 %copy-done.2 = f32[32,4,24]{0,2,1:T(8,128)S(1)} copy-done((f32[32,4,24]{0,2,1:T(8,128)S(1)}, f32[32,4,24]{0,2,1:T(8,128)}, u32[]{:S(2)}) %copy-start.2) | copy-done | bytes 12312
  6.8 0.0 copy-start.3
  6.8 0.0 copy-start.4
  6.9 0.0 copy-start.5
  6.9 0.0 copy-start.6
  6.9 0.7 %shard_map.103.code_any = f32[32,128]{1,0:T(8,128)} custom-call(f32[4,24,32]{2,1,0:T(8,128)S(1)} %bitcast.16), custom_call_target="tpu_custom_call" | custom-call | tf_op jit(solution)/shard_map/pallas_call | solution.py:333
  7.5 0.0 collective-permute-done.1.inner_ref
  7.5 0.0 collective-permute-done.2.outer_ref
  7.5 0.1 shard_map.104
  7.6 3.1 %collective-permute-start.3 = (bf16[2,2,128,128]{3,2,1,0:T(8,128)(2,1)S(1)}, bf16[2,2,128,128]{3,2,1,0:T(8,128)(2,1)S(1)}, u32[]{:S(2)}, u32[]{:S(2)}) collective-permute-start(bf16[2,2,128,128]{3,2,1,0:T(8,128)(2,1)S(1)} %get-tuple-element.22), channel_id=1, source_target_pairs={{0,8},{8,16},{16,24},{24,32},{32,40},{40,48},{48,56},{56,64},{64,7... | collective-permute-start | bytes 393224 | tf_op jit(solution)/shard_map/ppermute | solution.py:337
  10.7 11.1 %all-to-all-start = ((f32[32,1,128]{2,1,0:T(1,128)}), f32[32,1,128]{2,1,0:T(1,128)S(1)}, u32[]{:S(2)}, u32[]{:S(2)}) async-start(f32[32,1,128]{2,1,0:T(1,128)} %bitcast.8), calls=%async_computation | async-start | bytes 32768 | tf_op jit(solution)/shard_map/all_to_all | solution.py:338
  21.8 0.0 collective-permute-done.3.rim_ref
  21.8 0.0 collective-permute-done.earlier_ref
  21.9 0.0 copy-done
  21.9 0.0 copy-done.3
  21.9 0.0 copy-done.4
  21.9 0.0 copy-done.5
  21.9 0.0 copy-done.6
  21.9 3.8 %shard_map.106 = (f32[2608,128]{1,0:T(8,128)S(1)}, f32[4,24,32]{2,1,0:T(8,128)}) custom-call(s32[1,6]{1,0:T(1,128)S(1)} %bitcast.19, s32[4,24,32]{2,1,0:T(8,128)S(1)} %bitcast.17, bf16[2,6,128,128]{3,2,1,0:T(8,128)(2,1)S(1)} %shard_map.105.early_ref.refs_0_, bf16[4,6,128,128]{3,2,1,0:T(8,128)(2,1)S(1)} %get-tuple-element.23.x_ref.refs_1_, ...), custom_call_target="tpu_custom_call" | custom-call | tf_op jit(solution)/shard_map/pallas_call | solution.py:341
  25.8 4.6 %all-to-all-done = f32[32,1,128]{2,1,0:T(1,128)S(1)} async-done(((f32[32,1,128]{2,1,0:T(1,128)}), f32[32,1,128]{2,1,0:T(1,128)S(1)}, u32[]{:S(2)}, u32[]{:S(2)}) %all-to-all-start) | async-done | bytes 16416 | tf_op jit(solution)/shard_map/all_to_all | solution.py:338
  30.3 3.2 %shard_map.107 = (bf16[4,16,3584]{2,1,0:T(8,128)(2,1)S(1)}, bf16[384,2048]{1,0:T(8,128)(2,1)S(1)}, f32[8,128]{1,0:T(8,128)S(1)}) custom-call(bf16[2,6,128,128]{3,2,1,0:T(8,128)(2,1)S(1)} %shard_map.105.early_ref.refs_0_, bf16[4,6,128,128]{3,2,1,0:T(8,128)(2,1)S(1)} %get-tuple-element.23.x_ref.refs_1_, f32[2608,128]{1,0:T(8,128)S(1)} %get-tuple-element.25.refs_2_, ...), custom_call_target="tpu_custom_call" | custom-call | tf_op jit(solution)/shard_map/pallas_call | solution.py:356
  33.5 1.0 %collective-permute-start.4 = (bf16[4,16,3584]{2,1,0:T(8,128)(2,1)S(1)}, bf16[4,16,3584]{2,1,0:T(8,128)(2,1)S(1)}, u32[]{:S(2)}, u32[]{:S(2)}) collective-permute-start(bf16[4,16,3584]{2,1,0:T(8,128)(2,1)S(1)} %get-tuple-element.28), channel_id=1, source_target_pairs={{0,1},{1,0},{2,3},{3,2},{4,5},{5,4},{6,7},{7,6},{8,9},{9,8},{10,11... | collective-permute-start | bytes 1376264 | tf_op jit(solution)/shard_map/ppermute | solution.py:362
  34.6 1.2 %shard_map.108.mine_ref = f32[4,16,3584]{2,1,0:T(8,128)S(1)} custom-call(bf16[2,6,128,128]{3,2,1,0:T(8,128)(2,1)S(1)} %shard_map.105.early_ref.refs_0_, bf16[4,6,128,128]{3,2,1,0:T(8,128)(2,1)S(1)} %get-tuple-element.23.x_ref.refs_1_, bf16[384,2048]{1,0:T(8,128)(2,1)S(1)} %get-tuple-element.26.low_ref, f32[8,128]{1,0:T(8,128)S(1)} %get-tuple-element.27.small_ref), custom_call_target="tpu_custom_call" | custom-call | tf_op jit(solution)/shard_map/pallas_call | solution.py:363
  35.8 0.2 collective-permute-done.4.got_ref
  36.0 0.3 shard_map.109
  36.3 17.2 %all_to_all.15.parts_ref = bf16[16,16,1024]{2,1,0:T(8,128)(2,1)S(1)} all-to-all(bf16[16,16,1024]{2,1,0:T(8,128)(2,1)S(1)} %shard_map.109), channel_id=1, replica_groups=mesh['z'=8,'x'=4,'y'=4,'c'=2] {'x','y'}, dimensions={0} | all-to-all | bytes 1048576 | tf_op jit(solution)/shard_map/all_to_all | solution.py:365
  53.6 0.1 shard_map.110
  53.7 11.5 %all_to_all.16.parts_ref = f32[8,24,128]{2,1,0:T(8,128)S(1)} all-to-all(f32[8,24,128]{2,1,0:T(8,128)S(1)} %shard_map.110), channel_id=1, replica_groups=mesh['z'=8,'x'=4,'y'=4,'c'=2] {'z'}, dimensions={0} | all-to-all | bytes 196608 | tf_op jit(solution)/shard_map/all_to_all | solution.py:367
  65.2 0.6 shard_map.111
  (1 shorter events, 0.0 us)
Async XLA Ops:
  0.6 1.0 %copy-start.1 = (bf16[4,4,128,128]{3,2,1,0:T(8,128)(2,1)S(1)}, bf16[4,4,128,128]{3,2,1,0:T(8,128)(2,1)}, u32[]{:S(2)}) copy-start(bf16[4,4,128,128]{3,2,1,0:T(8,128)(2,1)} %frames_any.1) | copy-start | bytes 1572868
  1.7 20.2 %copy-start = (bf16[3456,128]{1,0:T(8,128)(2,1)S(1)}, bf16[3456,128]{1,0:T(8,128)(2,1)}, u32[]{:S(2)}) copy-start(bf16[3456,128]{1,0:T(8,128)(2,1)} %param.8) | copy-start | bytes 2654212
  1.9 5.7 %collective-permute-start.1 = (bf16[4,128,128]{2,1,0:T(8,128)(2,1)S(1)}, bf16[4,128,128]{2,1,0:T(8,128)(2,1)S(1)}, u32[]{:S(2)}, u32[]{:S(2)}) collective-permute-start(bf16[4,128,128]{2,1,0:T(8,128)(2,1)S(1)} %get-tuple-element.20), channel_id=1, source_target_pairs={{0,1},{1,0},{2,3},{3,2},{4,5},{5,4},{6,7},{7,6},{8,9},{9,8},{10,11... | collective-permute-start | bytes 393224 | tf_op jit(solution)/shard_map/ppermute | solution.py:332
  2.0 5.6 %collective-permute-start.2 = (bf16[4,128,128]{2,1,0:T(8,128)(2,1)S(1)}, bf16[4,128,128]{2,1,0:T(8,128)(2,1)S(1)}, u32[]{:S(2)}, u32[]{:S(2)}) collective-permute-start(bf16[4,128,128]{2,1,0:T(8,128)(2,1)S(1)} %get-tuple-element.21), channel_id=1, source_target_pairs={{1,2},{3,4},{5,6},{2,1},{4,3},{6,5},{9,10},{11,12},{13,14},{10,9},... | collective-permute-start | bytes 393224 | tf_op jit(solution)/shard_map/ppermute | solution.py:331
  2.6 19.2 %collective-permute-start = (bf16[2,4,128,128]{3,2,1,0:T(8,128)(2,1)S(1)}, bf16[2,4,128,128]{3,2,1,0:T(8,128)(2,1)S(1)}, u32[]{:S(2)}, u32[]{:S(2)}) collective-permute-start(bf16[2,4,128,128]{3,2,1,0:T(8,128)(2,1)S(1)} %get-tuple-element.18), channel_id=1, source_target_pairs={{0,8},{8,16},{16,24},{24,32},{32,40},{40,48},{48,56},{56,64},{64,7... | collective-permute-start | bytes 786440 | tf_op jit(solution)/shard_map/ppermute | solution.py:330
  6.0 0.8 %copy-start.2 = (f32[32,4,24]{0,2,1:T(8,128)S(1)}, f32[32,4,24]{0,2,1:T(8,128)}, u32[]{:S(2)}) copy-start(f32[32,4,24]{0,2,1:T(8,128)} %param.13) | copy-start | bytes 36868
  6.8 15.1 %copy-start.3 = (s32[32,4,24]{0,2,1:T(8,128)S(1)}, s32[32,4,24]{0,2,1:T(8,128)}, u32[]{:S(2)}) copy-start(s32[32,4,24]{0,2,1:T(8,128)} %param.12) | copy-start | bytes 36868
  6.8 15.1 %copy-start.4 = (f32[128,6]{0,1:T(8,128)S(1)}, f32[128,6]{0,1:T(8,128)}, u32[]{:S(2)}) copy-start(f32[128,6]{0,1:T(8,128)} %param.10) | copy-start | bytes 9220
  6.9 15.1 %copy-start.5 = (s32[6]{0:T(128)S(1)}, s32[6]{0:T(128)}, u32[]{:S(2)}) copy-start(s32[6]{0:T(128)} %param.11) | copy-start | bytes 76
  6.9 15.1 %copy-start.6 = (f32[128]{0:T(128)S(1)}, f32[128]{0:T(128)}, u32[]{:S(2)}) copy-start(f32[128]{0:T(128)} %param.9) | copy-start | bytes 1540
  7.6 14.2 %collective-permute-start.3 = (bf16[2,2,128,128]{3,2,1,0:T(8,128)(2,1)S(1)}, bf16[2,2,128,128]{3,2,1,0:T(8,128)(2,1)S(1)}, u32[]{:S(2)}, u32[]{:S(2)}) collective-permute-start(bf16[2,2,128,128]{3,2,1,0:T(8,128)(2,1)S(1)} %get-tuple-element.22), channel_id=1, source_target_pairs={{0,8},{8,16},{16,24},{24,32},{32,40},{40,48},{48,56},{56,64},{64,7... | collective-permute-start | bytes 393224 | tf_op jit(solution)/shard_map/ppermute | solution.py:337
  10.7 19.6 %all-to-all-start = ((f32[32,1,128]{2,1,0:T(1,128)}), f32[32,1,128]{2,1,0:T(1,128)S(1)}, u32[]{:S(2)}, u32[]{:S(2)}) async-start(f32[32,1,128]{2,1,0:T(1,128)} %bitcast.8), calls=%async_computation | async-start | bytes 32768 | tf_op jit(solution)/shard_map/all_to_all | solution.py:338
  33.5 2.5 %collective-permute-start.4 = (bf16[4,16,3584]{2,1,0:T(8,128)(2,1)S(1)}, bf16[4,16,3584]{2,1,0:T(8,128)(2,1)S(1)}, u32[]{:S(2)}, u32[]{:S(2)}) collective-permute-start(bf16[4,16,3584]{2,1,0:T(8,128)(2,1)S(1)} %get-tuple-element.28), channel_id=1, source_target_pairs={{0,1},{1,0},{2,3},{3,2},{4,5},{5,4},{6,7},{7,6},{8,9},{9,8},{10,11... | collective-permute-start | bytes 1376264 | tf_op jit(solution)/shard_map/ppermute | solution.py:362

commit v7 on v6

--- a/solution.py
+++ b/solution.py
@@ -127,6 +127,7 @@
     projection_ref,
     state_ref,
     quantized_ref,
+    wide_out_ref,
 ):
     rows, columns, groups = centres_ref.shape
     channel = lax.broadcasted_iota(jnp.int32, (columns, groups), 0) % L
@@ -142,14 +143,21 @@
     bias = bias_ref[...]
     pooled = [jnp.zeros((W, CH), f32) for _ in range(4)]
     for t in range(4):
+        left = jnp.concatenate(
+            [
+                jnp.concatenate([block(t + a, h + b) for a in range(3) for b in range(3)], 1)
+                for h in range(4)
+            ],
+            0,
+        )
+        wide_out_ref[...] = jnp.dot(left, wide, preferred_element_type=f32)
         for h in range(4):
-            left = jnp.concatenate([block(t + a, h + b) for a in range(3) for b in range(3)], 1)
-            z = jnp.dot(left, wide, preferred_element_type=f32)
+            rows_h = slice(h * W, (h + 1) * W)
             preact = (
                 bias
-                + shifted_rows(z[:, :CH], 1)
-                + z[:, CH : 2 * CH]
-                + shifted_rows(z[:, 2 * CH :], -1)
+                + shifted_rows(wide_out_ref[rows_h, :CH], 1)
+                + wide_out_ref[rows_h, CH : 2 * CH]
+                + shifted_rows(wide_out_ref[rows_h, 2 * CH :], -1)
             )
             sigmoid = 0.5 * jnp.tanh(0.5 * preact) + 0.5
             place = (t * 4 + h) * W
@@ -342,6 +350,7 @@
         forward_kernel,
         [shape((SMALL + 48, CH), f32), shape(centres.shape, f32)],
         [VMEM] * 7,
+        [pltpu.VMEM((4 * W, 3 * CH), f32)],
     )(
         levels.reshape(1, L),
         centres,

time: 67 us -> 67 us (level)
  no operation moved by 1% of the time
where the time goes in v7:
time: 67 us; the launch traced here: 65.8 us
  blocking collectives  28.7 us (43%)
  starting transfers between devices  19.4 us (29%)
  Pallas kernels  10.3 us (15%)
  waiting for transfers between devices  4.79 us (7%)
  local copies, waits for them, and re-layouts  1.85 us (3%)
  between operations  0.79 us (1%)
    all_to_all x1, blocking collectives, on_device(): chunks = lax.all_to_all(chunks, ('x', 'y'), 0, 0, tiled=True)  17.2 us
    all_to_all x1, blocking collectives, on_device(): parts = lax.all_to_all(chunks, 'z', 0, 0, tiled=True)  11.5 us
    all_to_all x1, starting transfers between devices, on_device(): lax.all_to_all(codes.reshape(shards, 1, CH), time_axes, 0, 0, tiled=True)  11.1 us
    all_to_all x1, waiting for transfers between devices, on_device(): lax.all_to_all(codes.reshape(shards, 1, CH), time_axes, 0, 0, tiled=True)  4.54 us
    pallas_call x1, Pallas kernels, on_device(): call(forward_kernel, [shape((SMALL + 48, CH), f32), shape(centres.shape,...  3.85 us
    ppermute x1, starting transfers between devices, on_device(): earlier = lax.ppermute(late, time_axes, later)  3.4 us
    pallas_call x1, Pallas kernels, on_device(): call(lambda *refs: backward_kernel(total_cells, *refs), [shape((4, 16, WI...  3.21 us
    ppermute x1, starting transfers between devices, on_device(): rim = lax.ppermute(rim, time_axes, later)  3.11 us
  transfers between devices with their start and end apart: 6, of which 2 were waited for; matrix products, arithmetic and copies ran while one was open for 0% of the time, Pallas kernels for 9%

profile of v7, /device:TPU:2, one launch (start us, length us, event | category | flops | bytes accessed | tf_op | source)
XLA Modules:
  0.0 65.8 jit_solution(1747753281181459407)
XLA Ops:
  0.6 0.0 copy-start.1
  0.6 1.0 %copy-done.1 = bf16[4,4,128,128]{3,2,1,0:T(8,128)(2,1)S(1)} copy-done((bf16[4,4,128,128]{3,2,1,0:T(8,128)(2,1)S(1)}, bf16[4,4,128,128]{3,2,1,0:T(8,128)(2,1)}, u32[]{:S(2)}) %copy-start.1) | copy-done | bytes 524312
  1.7 0.0 copy-start
  1.7 0.2 shard_map.102
  1.9 0.1 collective-permute-start.1
  2.0 0.7 %collective-permute-start.2 = (bf16[4,128,128]{2,1,0:T(8,128)(2,1)S(1)}, bf16[4,128,128]{2,1,0:T(8,128)(2,1)S(1)}, u32[]{:S(2)}, u32[]{:S(2)}) collective-permute-start(bf16[4,128,128]{2,1,0:T(8,128)(2,1)S(1)} %get-tuple-element.21), channel_id=1, source_target_pairs={{1,2},{3,4},{5,6},{2,1},{4,3},{6,5},{9,10},{11,12},{13,14},{10,9},... | collective-permute-start | bytes 393224 | tf_op jit(solution)/shard_map/ppermute | solution.py:339
  2.6 3.4 %collective-permute-start = (bf16[2,4,128,128]{3,2,1,0:T(8,128)(2,1)S(1)}, bf16[2,4,128,128]{3,2,1,0:T(8,128)(2,1)S(1)}, u32[]{:S(2)}, u32[]{:S(2)}) collective-permute-start(bf16[2,4,128,128]{3,2,1,0:T(8,128)(2,1)S(1)} %get-tuple-element.18), channel_id=1, source_target_pairs={{0,8},{8,16},{16,24},{24,32},{32,40},{40,48},{48,56},{56,64},{64,7... | collective-permute-start | bytes 786440 | tf_op jit(solution)/shard_map/ppermute | solution.py:338
  6.0 0.0 copy-start.2
  6.1 0.8 %copy-done.2 = f32[32,4,24]{0,2,1:T(8,128)S(1)} copy-done((f32[32,4,24]{0,2,1:T(8,128)S(1)}, f32[32,4,24]{0,2,1:T(8,128)}, u32[]{:S(2)}) %copy-start.2) | copy-done | bytes 12312
  6.8 0.0 copy-start.3
  6.8 0.0 copy-start.4
  6.9 0.0 copy-start.5
  6.9 0.0 copy-start.6
  6.9 0.7 %shard_map.103.code_any = f32[32,128]{1,0:T(8,128)} custom-call(f32[4,24,32]{2,1,0:T(8,128)S(1)} %bitcast.16), custom_call_target="tpu_custom_call" | custom-call | tf_op jit(solution)/shard_map/pallas_call | solution.py:341
  7.5 0.0 collective-permute-done.1.inner_ref
  7.5 0.0 collective-permute-done.2.outer_ref
  7.5 0.1 shard_map.104
  7.6 3.1 %collective-permute-start.3 = (bf16[2,2,128,128]{3,2,1,0:T(8,128)(2,1)S(1)}, bf16[2,2,128,128]{3,2,1,0:T(8,128)(2,1)S(1)}, u32[]{:S(2)}, u32[]{:S(2)}) collective-permute-start(bf16[2,2,128,128]{3,2,1,0:T(8,128)(2,1)S(1)} %get-tuple-element.22), channel_id=1, source_target_pairs={{0,8},{8,16},{16,24},{24,32},{32,40},{40,48},{48,56},{56,64},{64,7... | collective-permute-start | bytes 393224 | tf_op jit(solution)/shard_map/ppermute | solution.py:345
  10.7 11.1 %all-to-all-start = ((f32[32,1,128]{2,1,0:T(1,128)}), f32[32,1,128]{2,1,0:T(1,128)S(1)}, u32[]{:S(2)}, u32[]{:S(2)}) async-start(f32[32,1,128]{2,1,0:T(1,128)} %bitcast.8), calls=%async_computation | async-start | bytes 32768 | tf_op jit(solution)/shard_map/all_to_all | solution.py:346
  21.8 0.0 collective-permute-done.3.rim_ref
  21.8 0.0 collective-permute-done.earlier_ref
  21.9 0.0 copy-done
  21.9 0.0 copy-done.3
  21.9 0.0 copy-done.4
  21.9 0.0 copy-done.5
  21.9 0.0 copy-done.6
  21.9 3.9 %shard_map.106 = (f32[2608,128]{1,0:T(8,128)S(1)}, f32[4,24,32]{2,1,0:T(8,128)}) custom-call(s32[1,6]{1,0:T(1,128)S(1)} %bitcast.19, s32[4,24,32]{2,1,0:T(8,128)S(1)} %bitcast.17, bf16[2,6,128,128]{3,2,1,0:T(8,128)(2,1)S(1)} %shard_map.105.early_ref.refs_0_, bf16[4,6,128,128]{3,2,1,0:T(8,128)(2,1)S(1)} %get-tuple-element.23.x_ref.refs_1_, ...), custom_call_target="tpu_custom_call" | custom-call | tf_op jit(solution)/shard_map/pallas_call | solution.py:349
  25.8 4.5 %all-to-all-done = f32[32,1,128]{2,1,0:T(1,128)S(1)} async-done(((f32[32,1,128]{2,1,0:T(1,128)}), f32[32,1,128]{2,1,0:T(1,128)S(1)}, u32[]{:S(2)}, u32[]{:S(2)}) %all-to-all-start) | async-done | bytes 16416 | tf_op jit(solution)/shard_map/all_to_all | solution.py:346
  30.3 3.2 %shard_map.107 = (bf16[4,16,3584]{2,1,0:T(8,128)(2,1)S(1)}, bf16[384,2048]{1,0:T(8,128)(2,1)S(1)}, f32[8,128]{1,0:T(8,128)S(1)}) custom-call(bf16[2,6,128,128]{3,2,1,0:T(8,128)(2,1)S(1)} %shard_map.105.early_ref.refs_0_, bf16[4,6,128,128]{3,2,1,0:T(8,128)(2,1)S(1)} %get-tuple-element.23.x_ref.refs_1_, f32[2608,128]{1,0:T(8,128)S(1)} %get-tuple-element.25.refs_2_, ...), custom_call_target="tpu_custom_call" | custom-call | tf_op jit(solution)/shard_map/pallas_call | solution.py:365
  33.5 1.0 %collective-permute-start.4 = (bf16[4,16,3584]{2,1,0:T(8,128)(2,1)S(1)}, bf16[4,16,3584]{2,1,0:T(8,128)(2,1)S(1)}, u32[]{:S(2)}, u32[]{:S(2)}) collective-permute-start(bf16[4,16,3584]{2,1,0:T(8,128)(2,1)S(1)} %get-tuple-element.28), channel_id=1, source_target_pairs={{0,1},{1,0},{2,3},{3,2},{4,5},{5,4},{6,7},{7,6},{8,9},{9,8},{10,11... | collective-permute-start | bytes 1376264 | tf_op jit(solution)/shard_map/ppermute | solution.py:371
  34.6 1.2 %shard_map.108.mine_ref = f32[4,16,3584]{2,1,0:T(8,128)S(1)} custom-call(bf16[2,6,128,128]{3,2,1,0:T(8,128)(2,1)S(1)} %shard_map.105.early_ref.refs_0_, bf16[4,6,128,128]{3,2,1,0:T(8,128)(2,1)S(1)} %get-tuple-element.23.x_ref.refs_1_, bf16[384,2048]{1,0:T(8,128)(2,1)S(1)} %get-tuple-element.26.low_ref, f32[8,128]{1,0:T(8,128)S(1)} %get-tuple-element.27.small_ref), custom_call_target="tpu_custom_call" | custom-call | tf_op jit(solution)/shard_map/pallas_call | solution.py:372
  35.8 0.2 collective-permute-done.4.got_ref
  36.0 0.3 shard_map.109
  36.3 17.2 %all_to_all.15.parts_ref = bf16[16,16,1024]{2,1,0:T(8,128)(2,1)S(1)} all-to-all(bf16[16,16,1024]{2,1,0:T(8,128)(2,1)S(1)} %shard_map.109), channel_id=1, replica_groups=mesh['z'=8,'x'=4,'y'=4,'c'=2] {'x','y'}, dimensions={0} | all-to-all | bytes 1048576 | tf_op jit(solution)/shard_map/all_to_all | solution.py:374
  53.6 0.1 shard_map.110
  53.7 11.5 %all_to_all.16.parts_ref = f32[8,24,128]{2,1,0:T(8,128)S(1)} all-to-all(f32[8,24,128]{2,1,0:T(8,128)S(1)} %shard_map.110), channel_id=1, replica_groups=mesh['z'=8,'x'=4,'y'=4,'c'=2] {'z'}, dimensions={0} | all-to-all | bytes 196608 | tf_op jit(solution)/shard_map/all_to_all | solution.py:376
  65.2 0.6 shard_map.111
  (1 shorter events, 0.0 us)
Async XLA Ops:
  0.6 1.0 %copy-start.1 = (bf16[4,4,128,128]{3,2,1,0:T(8,128)(2,1)S(1)}, bf16[4,4,128,128]{3,2,1,0:T(8,128)(2,1)}, u32[]{:S(2)}) copy-start(bf16[4,4,128,128]{3,2,1,0:T(8,128)(2,1)} %frames_any.1) | copy-start | bytes 1572868
  1.7 20.2 %copy-start = (bf16[3456,128]{1,0:T(8,128)(2,1)S(1)}, bf16[3456,128]{1,0:T(8,128)(2,1)}, u32[]{:S(2)}) copy-start(bf16[3456,128]{1,0:T(8,128)(2,1)} %param.8) | copy-start | bytes 2654212
  1.9 5.7 %collective-permute-start.1 = (bf16[4,128,128]{2,1,0:T(8,128)(2,1)S(1)}, bf16[4,128,128]{2,1,0:T(8,128)(2,1)S(1)}, u32[]{:S(2)}, u32[]{:S(2)}) collective-permute-start(bf16[4,128,128]{2,1,0:T(8,128)(2,1)S(1)} %get-tuple-element.20), channel_id=1, source_target_pairs={{0,1},{1,0},{2,3},{3,2},{4,5},{5,4},{6,7},{7,6},{8,9},{9,8},{10,11... | collective-permute-start | bytes 393224 | tf_op jit(solution)/shard_map/ppermute | solution.py:340
  2.0 5.6 %collective-permute-start.2 = (bf16[4,128,128]{2,1,0:T(8,128)(2,1)S(1)}, bf16[4,128,128]{2,1,0:T(8,128)(2,1)S(1)}, u32[]{:S(2)}, u32[]{:S(2)}) collective-permute-start(bf16[4,128,128]{2,1,0:T(8,128)(2,1)S(1)} %get-tuple-element.21), channel_id=1, source_target_pairs={{1,2},{3,4},{5,6},{2,1},{4,3},{6,5},{9,10},{11,12},{13,14},{10,9},... | collective-permute-start | bytes 393224 | tf_op jit(solution)/shard_map/ppermute | solution.py:339
  2.6 19.2 %collective-permute-start = (bf16[2,4,128,128]{3,2,1,0:T(8,128)(2,1)S(1)}, bf16[2,4,128,128]{3,2,1,0:T(8,128)(2,1)S(1)}, u32[]{:S(2)}, u32[]{:S(2)}) collective-permute-start(bf16[2,4,128,128]{3,2,1,0:T(8,128)(2,1)S(1)} %get-tuple-element.18), channel_id=1, source_target_pairs={{0,8},{8,16},{16,24},{24,32},{32,40},{40,48},{48,56},{56,64},{64,7... | collective-permute-start | bytes 786440 | tf_op jit(solution)/shard_map/ppermute | solution.py:338
  6.0 0.8 %copy-start.2 = (f32[32,4,24]{0,2,1:T(8,128)S(1)}, f32[32,4,24]{0,2,1:T(8,128)}, u32[]{:S(2)}) copy-start(f32[32,4,24]{0,2,1:T(8,128)} %param.13) | copy-start | bytes 36868
  6.8 15.1 %copy-start.3 = (s32[32,4,24]{0,2,1:T(8,128)S(1)}, s32[32,4,24]{0,2,1:T(8,128)}, u32[]{:S(2)}) copy-start(s32[32,4,24]{0,2,1:T(8,128)} %param.12) | copy-start | bytes 36868
  6.8 15.1 %copy-start.4 = (f32[128,6]{0,1:T(8,128)S(1)}, f32[128,6]{0,1:T(8,128)}, u32[]{:S(2)}) copy-start(f32[128,6]{0,1:T(8,128)} %param.10) | copy-start | bytes 9220
  6.9 15.1 %copy-start.5 = (s32[6]{0:T(128)S(1)}, s32[6]{0:T(128)}, u32[]{:S(2)}) copy-start(s32[6]{0:T(128)} %param.11) | copy-start | bytes 76
  6.9 15.1 %copy-start.6 = (f32[128]{0:T(128)S(1)}, f32[128]{0:T(128)}, u32[]{:S(2)}) copy-start(f32[128]{0:T(128)} %param.9) | copy-start | bytes 1540
  7.6 14.2 %collective-permute-start.3 = (bf16[2,2,128,128]{3,2,1,0:T(8,128)(2,1)S(1)}, bf16[2,2,128,128]{3,2,1,0:T(8,128)(2,1)S(1)}, u32[]{:S(2)}, u32[]{:S(2)}) collective-permute-start(bf16[2,2,128,128]{3,2,1,0:T(8,128)(2,1)S(1)} %get-tuple-element.22), channel_id=1, source_target_pairs={{0,8},{8,16},{16,24},{24,32},{32,40},{40,48},{48,56},{56,64},{64,7... | collective-permute-start | bytes 393224 | tf_op jit(solution)/shard_map/ppermute | solution.py:345
  10.7 19.6 %all-to-all-start = ((f32[32,1,128]{2,1,0:T(1,128)}), f32[32,1,128]{2,1,0:T(1,128)S(1)}, u32[]{:S(2)}, u32[]{:S(2)}) async-start(f32[32,1,128]{2,1,0:T(1,128)} %bitcast.8), calls=%async_computation | async-start | bytes 32768 | tf_op jit(solution)/shard_map/all_to_all | solution.py:346
  33.5 2.5 %collective-permute-start.4 = (bf16[4,16,3584]{2,1,0:T(8,128)(2,1)S(1)}, bf16[4,16,3584]{2,1,0:T(8,128)(2,1)S(1)}, u32[]{:S(2)}, u32[]{:S(2)}) collective-permute-start(bf16[4,16,3584]{2,1,0:T(8,128)(2,1)S(1)} %get-tuple-element.28), channel_id=1, source_target_pairs={{0,1},{1,0},{2,3},{3,2},{4,5},{5,4},{6,7},{7,6},{8,9},{9,8},{10,11... | collective-permute-start | bytes 1376264 | tf_op jit(solution)/shard_map/ppermute | solution.py:371
